TPU v7x, 256 devices: a whole 4x4x8 slice. The times are simulated.
256 devices in a mesh: dp: 8 (over y, core), graph: 32 (over x, z).
Axes of the slice: x: 4, y: 4, z: 8, core: 2. Of those that a mesh axis runs over, the one named last changes fastest.
Arguments:
- node_latents: bfloat16 [8, 4096, 512], P('dp', 'graph'), may hold values from -6 to 6
- edge_latents: bfloat16 [8, 256, 128, 512], P('dp', 'graph'), may hold values from -6 to 6
- senders: int32 [256, 128], P('graph'), may hold values from 0 to 4095, as said below
- receivers: int32 [256, 128], P('graph'), may hold values from 0 to 4095, as said below
- block_counts: int32 [32], P('graph'), may hold values from 1 to 8, 128 in all
- edge_first: bfloat16 [3, 512, 512], replicated, may hold values from -0.25 to 0.25
- edge_second: bfloat16 [512, 512], replicated, may hold values from -0.25 to 0.25
- node_first: bfloat16 [2, 512, 512], replicated, may hold values from -0.25 to 0.25
- node_second: bfloat16 [512, 512], replicated, may hold values from -0.25 to 0.25
- vectors: float32 [4, 512], replicated, may hold values from 0.1 to 1.9
- node_cotangent: bfloat16 [8, 4096, 512], P('dp', 'graph'), may hold values from -6 to 6
- edge_cotangent: bfloat16 [8, 256, 128, 512], P('dp', 'graph'), may hold values from -6 to 6
Outputs:
- new_nodes: bfloat16 [8, 4096, 512], P('dp', 'graph')
- new_edges: bfloat16 [8, 256, 128, 512], P('dp', 'graph')
- node_grad: bfloat16 [8, 4096, 512], P('dp', 'graph')
- edge_grad: bfloat16 [8, 256, 128, 512], P('dp', 'graph')
- grad_edge_first: float32 [3, 512, 512], P(None, 'graph')
- grad_edge_second: float32 [512, 512], P('graph')
- grad_node_first: float32 [2, 512, 512], P(None, 'graph')
- grad_node_second: float32 [512, 512], P('graph')
- grad_vectors: float32 [4, 512], P(None, 'graph')
Inputs may be any that keep to these rules, and one draw needn't show every extreme that they name: `senders`: exactly 8 * 128 // 32 of the edges of blocks d * 8 to d * 8 + 7 have their sender among nodes o * 128 to o * 128 + 127, for every d and o (a sender node may repeat). Edges of block b have receivers among nodes (b // 8) * 128 to (b // 8) * 128 + 127. `block_counts`: the counts sum to 128; some device has all 8 blocks live.
All inputs are finite; a program needn't handle non-finite values.
Results may differ from a plain program's by a relative error of at most 0.027.
Values may be sent and summed in bfloat16 or wider, within the bound.
A program may use at most 128 MiB of HBM per device.

v0:
```python
import jax
import jax.numpy as jnp
from jax import lax
from jax.sharding import PartitionSpec as P

EPSILON = 1e-05


def product(left, right):
    return jnp.dot(left, right, preferred_element_type=jnp.float32)


def product_back(left, right):
    return lax.dot_general(
        left, right, (((1,), (1,)), ((), ())), preferred_element_type=jnp.float32
    )


def product_over(left, right):
    return lax.dot_general(
        left, right, (((0,), (0,)), ((), ())), preferred_element_type=jnp.float32
    )


def norm_forward(values, scales):
    average = jnp.mean(values, -1, keepdims=True)
    centered = values - average
    inverse = lax.rsqrt(jnp.mean(centered * centered, -1, keepdims=True) + EPSILON)
    normed = centered * inverse
    return (normed * scales, normed, inverse)


def norm_backward(upstream, normed, inverse, scales):
    scaled = upstream * scales
    return inverse * (
        scaled
        - jnp.mean(scaled, -1, keepdims=True)
        - normed * jnp.mean(scaled * normed, -1, keepdims=True)
    )


def silu_slope(values):
    sigmoid = jax.nn.sigmoid(values)
    return sigmoid * (1.0 + values * (1.0 - sigmoid))


def body(
    node_latents,
    edge_latents,
    senders,
    receivers,
    block_counts,
    edge_first,
    edge_second,
    node_first,
    node_second,
    vectors,
    node_cotangent,
    edge_cotangent,
):
    node_rows = node_latents[0]
    own_count, latent_width = node_rows.shape
    blocks, block_rows = senders.shape
    edge_total = blocks * block_rows
    flat_edges = edge_latents[0].reshape(edge_total, latent_width)
    flat_cot = edge_cotangent[0].reshape(edge_total, latent_width).astype(jnp.float32)
    send_index = senders.reshape(-1)
    first_node = lax.axis_index("graph") * own_count
    local_recv = receivers - first_node
    onehot = (
        local_recv[:, None, :] == jnp.arange(own_count, dtype=jnp.int32)[None, :, None]
    ).astype(jnp.bfloat16)
    live_blocks = (jnp.arange(blocks, dtype=jnp.int32) < block_counts[0]).astype(jnp.float32)
    live_rows = jnp.broadcast_to(live_blocks[:, None], (blocks, block_rows)).reshape(-1, 1)
    all_nodes = lax.all_gather(node_latents, "graph", axis=1, tiled=True)[0]
    sent_rows = jnp.take(all_nodes, send_index, axis=0)
    recv_rows = (
        jnp.einsum("bne,nd->bed", onehot, node_rows, preferred_element_type=jnp.float32)
        .astype(jnp.bfloat16)
        .reshape(edge_total, latent_width)
    )
    edge_pre = (
        product(flat_edges, edge_first[0])
        + product(sent_rows, edge_first[1])
        + product(recv_rows, edge_first[2])
        + vectors[0]
    )
    edge_act = jax.nn.silu(edge_pre).astype(jnp.bfloat16)
    message, edge_normed, edge_inverse = norm_forward(product(edge_act, edge_second), vectors[2])
    message_b = (live_rows * message).astype(jnp.bfloat16)
    new_edges = (flat_edges.astype(jnp.float32) + message_b.astype(jnp.float32)).astype(
        jnp.bfloat16
    )
    aggregate = jnp.einsum(
        "bne,bed->nd",
        onehot,
        message_b.reshape(blocks, block_rows, latent_width),
        preferred_element_type=jnp.float32,
    ).astype(jnp.bfloat16)
    node_pre = product(node_rows, node_first[0]) + product(aggregate, node_first[1]) + vectors[1]
    node_act = jax.nn.silu(node_pre).astype(jnp.bfloat16)
    node_out, node_normed, node_inverse = norm_forward(product(node_act, node_second), vectors[3])
    new_nodes = (node_rows.astype(jnp.float32) + node_out).astype(jnp.bfloat16)
    upstream = node_cotangent[0].astype(jnp.float32)
    node_dz = norm_backward(upstream, node_normed, node_inverse, vectors[3]).astype(jnp.bfloat16)
    node_dpre = (product_back(node_dz, node_second) * silu_slope(node_pre)).astype(jnp.bfloat16)
    aggregate_cot = product_back(node_dpre, node_first[1]).astype(jnp.bfloat16)
    recv_cot = jnp.einsum(
        "bne,nd->bed", onehot, aggregate_cot, preferred_element_type=jnp.float32
    ).reshape(edge_total, latent_width)
    message_cot = live_rows * (flat_cot + recv_cot)
    edge_dz = norm_backward(message_cot, edge_normed, edge_inverse, vectors[2]).astype(jnp.bfloat16)
    edge_dpre = (product_back(edge_dz, edge_second) * silu_slope(edge_pre)).astype(jnp.bfloat16)
    edge_grad = (flat_cot + product_back(edge_dpre, edge_first[0])).astype(jnp.bfloat16)
    dense_send = jax.ops.segment_sum(
        product_back(edge_dpre, edge_first[1]), send_index, num_segments=all_nodes.shape[0]
    )
    from_send = lax.psum_scatter(
        dense_send.astype(jnp.bfloat16), "graph", scatter_dimension=0, tiled=True
    ).astype(jnp.float32)
    from_recv = jax.ops.segment_sum(
        product_back(edge_dpre, edge_first[2]), local_recv.reshape(-1), num_segments=own_count
    )
    node_grad = (upstream + product_back(node_dpre, node_first[0]) + from_send + from_recv).astype(
        jnp.bfloat16
    )
    matrices = jnp.stack(
        [
            product_over(flat_edges, edge_dpre),
            product_over(sent_rows, edge_dpre),
            product_over(recv_rows, edge_dpre),
            product_over(edge_act, edge_dz),
            product_over(node_rows, node_dpre),
            product_over(aggregate, node_dpre),
            product_over(node_act, node_dz),
        ]
    )
    columns = jnp.stack(
        [
            jnp.sum(edge_dpre.astype(jnp.float32), 0),
            jnp.sum(node_dpre.astype(jnp.float32), 0),
            jnp.sum(message_cot * edge_normed, 0),
            jnp.sum(upstream * node_normed, 0),
        ]
    )
    matrices, columns = (
        lax.psum(matrices.astype(jnp.bfloat16), "dp").astype(jnp.float32),
        lax.psum(columns.astype(jnp.bfloat16), "dp").astype(jnp.float32),
    )
    matrices, columns = (
        lax.psum_scatter(
            matrices.astype(jnp.bfloat16), "graph", scatter_dimension=1, tiled=True
        ).astype(jnp.float32),
        lax.psum_scatter(
            columns.astype(jnp.bfloat16), "graph", scatter_dimension=1, tiled=True
        ).astype(jnp.float32),
    )
    return (
        new_nodes[None],
        new_edges.reshape(1, blocks, block_rows, latent_width),
        node_grad[None],
        edge_grad.reshape(1, blocks, block_rows, latent_width),
        matrices[0:3],
        matrices[3],
        matrices[4:6],
        matrices[6],
        columns,
    )


def solution(mesh):
    return jax.shard_map(
        body,
        mesh=mesh,
        in_specs=(
            P("dp", "graph", None),
            P("dp", "graph", None, None),
            P("graph", None),
            P("graph", None),
            P("graph"),
            P(),
            P(),
            P(),
            P(),
            P(),
            P("dp", "graph", None),
            P("dp", "graph", None, None),
        ),
        out_specs=(
            P("dp", "graph", None),
            P("dp", "graph", None, None),
            P("dp", "graph", None),
            P("dp", "graph", None, None),
            P(None, "graph", None),
            P("graph", None),
            P(None, "graph", None),
            P("graph", None),
            P(None, "graph"),
        ),
        check_vma=False,
    )
```

profile of v0, /device:TPU:1, one launch (start us, length us, event | category | flops | bytes accessed | tf_op | source)
XLA Modules:
  0.0 855.2 jit_solution(9088620935405088356)
XLA Ops:
  13.1 2.5 convolution_convert_fusion
  15.5 1.7 fusion.38
  17.3 76.3 %all-gather.2.cloned.1.call-done = bf16[1,4096,512]{2,1,0:T(8,128)(2,1)} async-done(((bf16[1,128,512]{2,1,0:T(8,128)(2,1)}), bf16[1,4096,512]{2,1,0:T(8,128)(2,1)}) %all-gather.2.cloned.1.call-update) | async-done | bytes 4194320 | tf_op jit(solution)/shard_map/all_gather | solution.py:75
  93.6 7.8 gather_fusion
  101.4 2.2 fusion.35
  103.6 1.8 add_add_fusion
  108.0 1.6 add_convert_fusion
  112.3 3.4 fusion.4
  115.8 2.6 multiply_reduce_fusion
  123.1 1.6 fusion.10
  124.7 1.6 fusion.12
  126.3 1.7 fusion.14
  131.5 7.9 copy.37
  140.5 214.9 %reduce-scatter.8.cloned.1.call-done = bf16[7,16,512]{2,0,1:T(8,128)(2,1)} async-done(((bf16[7,512,512]{2,0,1:T(8,128)(2,1)}), bf16[7,16,512]{2,0,1:T(8,128)(2,1)}) %reduce-scatter.8.cloned.1.call-update) | async-done | bytes 114704 | tf_op jit(solution)/shard_map/reduce_scatter | solution.py:151
  355.6 3.2 fusion.33
  358.8 11.0 %scatter_custom_fusion = f32[4096,512]{1,0:T(8,128)} fusion(s32[1024]{0:T(1024)} %bitcast.192, f32[1024,512]{1,0:T(8,128)} %fusion.33, f32[]{:T(128)} %constant.44.clone.1), kind=kCustom, calls=%fused_computation.3 | custom fusion | flops 524288 | bytes 8389120 | tf_op jit(solution)/shard_map/scatter-add | solution.py:115
  369.8 5.9 convert_element_type.123
  376.3 2.2 fusion.30
  378.6 2.8 fusion.6
  381.4 169.0 %reduce-scatter.10.cloned.1.call-done = bf16[16,4]{1,0:T(8,128)(2,1)} async-done(((bf16[512,4]{1,0:T(8,128)(2,1)}), bf16[16,4]{1,0:T(8,128)(2,1)}) %reduce-scatter.10.cloned.1.call-update) | async-done | bytes 144
  551.2 17.9 %psum.17 = bf16[4,16]{1,0:T(4,128)(2,1)S(1)} all-reduce(bf16[4,16]{1,0:T(4,128)(2,1)S(1)} %copy.47), channel_id=1, replica_groups=mesh['dp'=8,'graph'=32] {'dp'}, use_global_device_ids=true, to_apply=%region_17.18 | all-reduce | flops 64 | bytes 256 | tf_op jit(solution)/shard_map/psum | solution.py:148
  569.6 49.1 %all-reduce.2.cloned.1.call-done = bf16[7,16,512]{2,0,1:T(8,128)(2,1)} async-done(((bf16[7,16,512]{2,0,1:T(8,128)(2,1)}), bf16[7,16,512]{2,0,1:T(8,128)(2,1)}) %all-reduce.2.cloned.1.call-update) | async-done | bytes 114704 | tf_op jit(solution)/shard_map/psum | solution.py:147
  624.2 215.8 %reduce-scatter.6.cloned.1.call-done = bf16[128,512]{1,0:T(8,128)(2,1)} async-done(((bf16[4096,512]{1,0:T(8,128)(2,1)}), bf16[128,512]{1,0:T(8,128)(2,1)}) %reduce-scatter.6.cloned.1.call-update) | async-done | bytes 131088 | tf_op jit(solution)/shard_map/reduce_scatter | solution.py:118
  841.3 6.7 scatter_fusion
  (99 shorter events, 29.3 us)
Async XLA Ops:
  7.2 98.2 %copy-start = (bf16[512,512]{1,0:T(8,128)(2,1)S(1)}, bf16[512,512]{1,0:T(8,128)(2,1)}, u32[]{:S(2)}) copy-start(bf16[512,512]{1,0:T(8,128)(2,1)} %param.18) | copy-start | bytes 1572868
  7.2 86.4 %all-gather.2.cloned.1.call-start = ((), (), s32[]{:S(2)}) async-start(), calls=%async_computation.3 | async-start | bytes 4325376 | tf_op jit(solution)/shard_map/all_gather | solution.py:75
  7.9 347.4 %reduce-scatter.8.cloned.1.call-start = ((), (), s32[]{:S(2)}) async-start(), calls=%async_computation.5 | async-start | bytes 4325376 | tf_op jit(solution)/shard_map/reduce_scatter | solution.py:151
  8.6 6.9 copy-start.9
  101.4 2.2 copy-start.6
  105.4 1.4 copy-start.13
  106.8 1.2 copy-start.10
  108.0 2.2 copy-start.8
  109.6 1.6 copy-start.12
  109.6 1.6 copy-start.16
  110.6 1.7 copy-start.17
  115.8 2.6 copy-start.1
  115.8 2.8 copy-start.2
  118.6 1.6 copy-start.14
  120.2 1.3 copy-start.11
  121.5 234.2 %copy-start.4 = (bf16[1024,512]{1,0:T(8,128)(2,1)}, bf16[1024,512]{1,0:T(8,128)(2,1)S(1)}, u32[]{:S(2)}) copy-start(bf16[1024,512]{1,0:T(8,128)(2,1)S(1)} %get-tuple-element.50) | copy-start | bytes 3145732
  121.5 1.6 copy-start.15
  123.1 1.6 copy-start.7
  126.3 4.0 copy-start.18
  139.5 410.9 %reduce-scatter.10.cloned.1.call-start = ((), (), s32[]{:S(2)}) async-start(), calls=%async_computation.7 | async-start | bytes 135168
  140.4 478.3 %all-reduce.2.cloned.1.call-start = ((), (), s32[]{:S(2)}) async-start(), calls=%async_computation.6 | async-start | bytes 262144 | tf_op jit(solution)/shard_map/psum | solution.py:147
  355.4 484.6 %reduce-scatter.6.cloned.1.call-start = ((), (), s32[]{:S(2)}) async-start(), calls=%async_computation.4 | async-start | bytes 4325376 | tf_op jit(solution)/shard_map/reduce_scatter | solution.py:118
  376.3 2.3 copy-start.3
  376.3 2.3 copy-start.5
  (2 other events, 1.7 us)
Sparse Core Ops, SparseCore 0:
  10.6 82.8 all-gather.1
  139.6 215.7 reduce-scatter.7
  360.0 190.3 reduce-scatter.9
  552.6 66.1 all-reduce.1
  623.0 216.9 reduce-scatter.5
where the time goes:
time: 860 us; the launch traced here: 855 us
  waiting for transfers between devices  726 us (84%)
  matrix products  36.1 us (4%)
  other arithmetic  33.9 us (4%)
  local copies, waits for them, and re-layouts  26.5 us (3%)
  blocking collectives  17.9 us (2%)
  between operations  14.8 us (2%)
    reduce_scatter x1, waiting for transfers between devices, body(): lax.psum_scatter(dense_send.astype(jnp.bfloat16), 'graph', scatter_dimens...  216 us
    reduce_scatter x1, waiting for transfers between devices, body(): lax.psum_scatter(matrices.astype(jnp.bfloat16), 'graph', scatter_dimensio...  215 us
    unnamed x6, waiting for transfers between devices  170 us
    all_gather x1, waiting for transfers between devices, body(): all_nodes = lax.all_gather(node_latents, 'graph', axis=1, tiled=True)[0]  76.3 us
    psum x1, waiting for transfers between devices, body(): lax.psum(matrices.astype(jnp.bfloat16), 'dp').astype(jnp.float32)  49.1 us
    psum x1, blocking collectives, body(): lax.psum(columns.astype(jnp.bfloat16), 'dp').astype(jnp.float32)  17.9 us
  transfers between devices with their start and end apart: 5, of which 5 were waited for; matrix products, arithmetic and copies ran while one was open for 5% of the time, Pallas kernels for 0%

commit v1 on v0

v1 whole, which is shorter than its diff:
```python
import jax
import jax.numpy as jnp
from jax import lax
from jax.experimental import pallas as pl
from jax.experimental.pallas import tpu as pltpu
from jax.sharding import PartitionSpec as P

EPSILON = 1e-05
MESH = pl.DeviceIdType.MESH
F32 = jnp.float32
BF16 = jnp.bfloat16

XN, ZN, YN = 4, 8, 4
GN = XN * ZN
ND = 128
D = 512
EDGES = 1024
SLOTS = 32
BM = 256
NB = EDGES // BM
VMEM_LIMIT = 56 * 1024 * 1024

RING_ORDER = (0, 1, 5, 2, 6, 3, 7, 4)
RING_OFFSET = (0, -1, -2, -3, -4, 1, 2, 3)


def nn(left, right):
    return jnp.dot(left, right, preferred_element_type=F32)


def nt(left, right):
    return lax.dot_general(left, right, (((1,), (1,)), ((), ())), preferred_element_type=F32)


def tn(left, right):
    return lax.dot_general(left, right, (((0,), (0,)), ((), ())), preferred_element_type=F32)


def place():
    dp = lax.axis_index("dp")
    graph = lax.axis_index("graph")
    return dp, graph // ZN, graph % ZN


def remote(src, dst, send, recv, device):
    return pltpu.make_async_remote_copy(
        src_ref=src, dst_ref=dst, send_sem=send, recv_sem=recv, device_id=device, device_id_type=MESH
    )


def enter(devices):
    barrier = pltpu.get_barrier_semaphore()
    for device in devices:
        pl.semaphore_signal(barrier, inc=1, device_id=device, device_id_type=MESH)
    pl.semaphore_wait(barrier, len(devices))


def onehot_rows(count, row):
    index = lax.broadcasted_iota(jnp.int32, (count, row.shape[1]), 0)
    return jnp.where(index == row, 1.0, 0.0).astype(BF16)


def exchange_kernel(
    node_ref,
    senders_ref,
    buf_ref,
    slot_ref,
    list_ref,
    ring,
    lists_own,
    lists_in,
    stage,
    ring_send,
    ring_recv,
    list_send,
    list_recv,
    x_send,
    x_recv,
):
    dp, x, z = place()
    up = (dp, x * ZN + (z + 1) % ZN)
    down = (dp, x * ZN + (z + ZN - 1) % ZN)
    peers = [None] + [(dp, ((x + k) % XN) * ZN + z) for k in range(1, XN)]
    enter([up, down] + peers[1:])

    def hop(src, slot, device):
        copy = remote(src, ring.at[slot], ring_send.at[slot], ring_recv.at[slot], device)
        copy.start()
        return copy

    hops = {1: hop(node_ref, 1, up), 5: hop(node_ref, 5, down)}

    senders = senders_ref[...]
    owners = senders // ND
    local = (senders % ND).astype(F32)
    earlier = jnp.where(
        lax.broadcasted_iota(jnp.int32, (ND, ND), 0) < lax.broadcasted_iota(jnp.int32, (ND, ND), 1), 1.0, 0.0
    ).astype(BF16)
    base = jnp.zeros((GN, 1), F32)
    table = jnp.zeros((GN, ND), F32)
    lane = lax.broadcasted_iota(jnp.int32, (ND, ND), 0)
    group = lax.broadcasted_iota(jnp.int32, (GN, ND), 0)
    for b in range(EDGES // ND):
        owner = owners[b : b + 1, :]
        mine = jnp.where(group == owner, 1.0, 0.0)
        before = nn(mine.astype(BF16), earlier) + base
        rank = jnp.sum(mine * before, axis=0, keepdims=True).astype(jnp.int32)
        base = base + jnp.sum(mine, axis=1, keepdims=True)
        slot_ref[b : b + 1, :] = owner * SLOTS + rank
        column = jnp.where(lane == rank + SLOTS * x, 1.0, 0.0).astype(BF16)
        table = table + nt((mine * local[b : b + 1, :]).astype(BF16), column)
    lists_own[...] = table.reshape(XN, ZN, ND)

    list_copies = []
    for k in range(1, XN):
        copy = remote(lists_own.at[(x + k) % XN], lists_in.at[k - 1], list_send.at[k - 1], list_recv.at[k - 1], peers[k])
        copy.start()
        list_copies.append(copy)
    for copy in list_copies:
        copy.wait_recv()
    list_ref[...] = (lists_own[x] + lists_in[0] + lists_in[1] + lists_in[2]).astype(jnp.int32)

    x_copies = []
    for place_of in RING_ORDER:
        source = (z + RING_OFFSET[place_of] + ZN) % ZN
        if place_of:
            hops[place_of].wait_recv()
            if place_of in (1, 2, 3):
                hops[place_of + 1] = hop(ring.at[place_of], place_of + 1, up)
            elif place_of in (5, 6):
                hops[place_of + 1] = hop(ring.at[place_of], place_of + 1, down)
            block = ring[place_of]
        else:
            block = node_ref[...]
        chosen = onehot_rows(ND, list_ref[pl.ds(source, 1), :])
        stage[place_of] = tn(chosen, block).astype(BF16).reshape(XN, SLOTS, D)
        buf_ref[x * ZN + source] = stage[place_of, x]
        for k in range(1, XN):
            copy = remote(
                stage.at[place_of, (x + k) % XN],
                buf_ref.at[x * ZN + source],
                x_send.at[place_of, k - 1],
                x_recv.at[place_of, k - 1],
                peers[k],
            )
            copy.start()
            x_copies.append(copy)
    for copy in x_copies:
        copy.wait_recv()
    for copy in list_copies + list(hops.values()) + x_copies:
        copy.wait_send()


def exchange(node_rows, senders):
    vmem = pl.BlockSpec(memory_space=pltpu.VMEM)
    return pl.pallas_call(
        exchange_kernel,
        out_shape=(
            jax.ShapeDtypeStruct((GN, SLOTS, D), BF16),
            jax.ShapeDtypeStruct((EDGES // ND, ND), jnp.int32),
            jax.ShapeDtypeStruct((ZN, ND), jnp.int32),
        ),
        in_specs=[vmem] * 2,
        out_specs=(vmem,) * 3,
        scratch_shapes=[
            pltpu.VMEM((ZN, ND, D), BF16),
            pltpu.VMEM((XN, ZN, ND), F32),
            pltpu.VMEM((XN - 1, ZN, ND), F32),
            pltpu.VMEM((ZN, XN, SLOTS, D), BF16),
            pltpu.SemaphoreType.DMA((ZN,)),
            pltpu.SemaphoreType.DMA((ZN,)),
            pltpu.SemaphoreType.DMA((XN - 1,)),
            pltpu.SemaphoreType.DMA((XN - 1,)),
            pltpu.SemaphoreType.DMA((ZN, XN - 1)),
            pltpu.SemaphoreType.DMA((ZN, XN - 1)),
        ],
        compiler_params=pltpu.CompilerParams(
            collective_id=0, has_side_effects=True, vmem_limit_bytes=VMEM_LIMIT
        ),
        name="exchange",
    )(node_rows, senders)


def normalize(values):
    average = jnp.mean(values, -1, keepdims=True)
    centered = values - average
    inverse = lax.rsqrt(jnp.mean(centered * centered, -1, keepdims=True) + EPSILON)
    return centered * inverse, inverse


def norm_backward(upstream, normed, inverse, scales):
    scaled = upstream * scales
    return inverse * (
        scaled
        - jnp.mean(scaled, -1, keepdims=True)
        - normed * jnp.mean(scaled * normed, -1, keepdims=True)
    )


def sigmoid(values):
    return 0.5 + 0.5 * jnp.tanh(0.5 * values)


def dense_kernel(
    counts_ref,
    node_ref,
    edge_ref,
    buf_ref,
    slot_ref,
    recv_ref,
    edge_first_ref,
    edge_second_ref,
    node_first_ref,
    node_second_ref,
    vectors_ref,
    node_cot_ref,
    edge_cot_ref,
    new_nodes_ref,
    new_edges_ref,
    edge_grad_ref,
    node_part_ref,
    back_ref,
    grads_ref,
    perm,
    recv_hot,
    act,
    slope,
    normed,
    inverse,
    dz,
    dpre,
):
    first_node = lax.axis_index("graph") * ND
    live_rows = counts_ref[0] * 128
    h = node_ref[...]
    h_recv = nn(h, edge_first_ref[2]).astype(BF16)
    aggregate = jnp.zeros((ND, D), F32)
    per = BM // 128
    for i in range(NB):
        rows = slice(i * BM, (i + 1) * BM)
        slot = jnp.concatenate([slot_ref[i * per + j : i * per + j + 1, :] for j in range(per)], axis=1)
        recv = jnp.concatenate([recv_ref[i * per + j : i * per + j + 1, :] for j in range(per)], axis=1)
        perm[:, rows] = onehot_rows(EDGES, slot)
        recv_hot[:, rows] = onehot_rows(ND, recv - first_node)
        sent = tn(perm[:, rows], buf_ref[...]).astype(BF16)
        e = edge_ref[rows, :]
        pre = (
            nn(e, edge_first_ref[0])
            + nn(sent, edge_first_ref[1])
            + tn(recv_hot[:, rows], h_recv)
            + vectors_ref[0:1, :]
        )
        gate = sigmoid(pre)
        act_b = (pre * gate).astype(BF16)
        act[rows, :] = act_b
        slope[rows, :] = gate * (1.0 + pre * (1.0 - gate))
        hat, inv = normalize(nn(act_b, edge_second_ref[...]))
        normed[rows, :] = hat
        inverse[rows, :] = inv
        live = lax.broadcasted_iota(jnp.int32, (BM, 1), 0) + i * BM < live_rows
        message = jnp.where(live, hat * vectors_ref[2:3, :], 0.0).astype(BF16)
        new_edges_ref[rows, :] = (e.astype(F32) + message.astype(F32)).astype(BF16)
        aggregate = aggregate + nn(recv_hot[:, rows], message)
    aggregate = aggregate.astype(BF16)

    node_pre = nn(h, node_first_ref[0]) + nn(aggregate, node_first_ref[1]) + vectors_ref[1:2, :]
    node_gate = sigmoid(node_pre)
    node_act = (node_pre * node_gate).astype(BF16)
    node_hat, node_inv = normalize(nn(node_act, node_second_ref[...]))
    new_nodes_ref[...] = (h.astype(F32) + node_hat * vectors_ref[3:4, :]).astype(BF16)
    upstream = node_cot_ref[...].astype(F32)
    node_dz = norm_backward(upstream, node_hat, node_inv, vectors_ref[3:4, :]).astype(BF16)
    node_dpre = (
        nt(node_dz, node_second_ref[...]) * (node_gate * (1.0 + node_pre * (1.0 - node_gate)))
    ).astype(BF16)
    aggregate_cot = nt(node_dpre, node_first_ref[1]).astype(BF16)

    col_edge = jnp.zeros((1, D), F32)
    col_scale = jnp.zeros((1, D), F32)
    received = jnp.zeros((ND, D), F32)
    back = jnp.zeros((EDGES, D), F32)
    for i in range(NB):
        rows = slice(i * BM, (i + 1) * BM)
        live = lax.broadcasted_iota(jnp.int32, (BM, 1), 0) + i * BM < live_rows
        cot = edge_cot_ref[rows, :].astype(F32)
        message_cot = jnp.where(live, cot + tn(recv_hot[:, rows], aggregate_cot), 0.0)
        hat = normed[rows, :]
        col_scale = col_scale + jnp.sum(message_cot * hat, 0, keepdims=True)
        dz_b = norm_backward(message_cot, hat, inverse[rows, :], vectors_ref[2:3, :]).astype(BF16)
        dz[rows, :] = dz_b
        dpre_b = (nt(dz_b, edge_second_ref[...]) * slope[rows, :]).astype(BF16)
        dpre[rows, :] = dpre_b
        col_edge = col_edge + jnp.sum(dpre_b.astype(F32), 0, keepdims=True)
        edge_grad_ref[rows, :] = (cot + nt(dpre_b, edge_first_ref[0])).astype(BF16)
        received = received + nn(recv_hot[:, rows], dpre_b)
    back_ref[...] = nn(perm[...], dpre[...]).astype(BF16)
    received = received.astype(BF16)
    node_part_ref[...] = upstream + nt(node_dpre, node_first_ref[0]) + nt(received, edge_first_ref[2])

    grads_ref[0] = tn(edge_ref[...], dpre[...]).astype(BF16)
    grads_ref[1] = tn(buf_ref[...], back_ref[...]).astype(BF16)
    grads_ref[2] = tn(h, received).astype(BF16)
    grads_ref[3] = tn(act[...], dz[...]).astype(BF16)
    grads_ref[4] = tn(h, node_dpre).astype(BF16)
    grads_ref[5] = tn(aggregate, node_dpre).astype(BF16)
    grads_ref[6] = tn(node_act, node_dz).astype(BF16)
    columns = jnp.concatenate(
        [
            col_edge,
            jnp.sum(node_dpre.astype(F32), 0, keepdims=True),
            col_scale,
            jnp.sum(upstream * node_hat, 0, keepdims=True),
            jnp.zeros((124, D), F32),
        ],
        axis=0,
    )
    grads_ref[7, :, 0:128] = columns.T.astype(BF16)
    grads_ref[7, :, 128:512] = jnp.zeros((D, 384), BF16)


def dense(counts, node, edges, buf, slot, recv, edge_first, edge_second, node_first, node_second, vectors, node_cot, edge_cot):
    vmem = pl.BlockSpec(memory_space=pltpu.VMEM)
    return pl.pallas_call(
        dense_kernel,
        out_shape=(
            jax.ShapeDtypeStruct((ND, D), BF16),
            jax.ShapeDtypeStruct((EDGES, D), BF16),
            jax.ShapeDtypeStruct((EDGES, D), BF16),
            jax.ShapeDtypeStruct((ND, D), F32),
            jax.ShapeDtypeStruct((EDGES, D), BF16),
            jax.ShapeDtypeStruct((8, D, D), BF16),
        ),
        in_specs=[pl.BlockSpec(memory_space=pltpu.SMEM)] + [vmem] * 12,
        out_specs=(vmem,) * 6,
        scratch_shapes=[
            pltpu.VMEM((EDGES, EDGES), BF16),
            pltpu.VMEM((ND, EDGES), BF16),
            pltpu.VMEM((EDGES, D), BF16),
            pltpu.VMEM((EDGES, D), F32),
            pltpu.VMEM((EDGES, D), F32),
            pltpu.VMEM((EDGES, 1), F32),
            pltpu.VMEM((EDGES, D), BF16),
            pltpu.VMEM((EDGES, D), BF16),
        ],
        compiler_params=pltpu.CompilerParams(vmem_limit_bytes=VMEM_LIMIT),
        name="dense",
    )(counts, node, edges, buf, slot, recv, edge_first, edge_second, node_first, node_second, vectors, node_cot, edge_cot)


REDUCE_ORDER = (4, 7, 3, 6, 2, 5, 1, 0)
REDUCE_OFFSET = (0, 1, 2, 3, 4, -1, -2, -3)


def reduce_kernel(
    back_ref,
    list_ref,
    grads_ref,
    node_part_ref,
    weight_ref,
    node_grad_ref,
    edge_first_ref,
    edge_second_ref,
    node_first_ref,
    node_second_ref,
    columns_ref,
    rows_in,
    ring_out,
    ring_in,
    core_in,
    pair,
    y_in,
    y_sum,
    x_in,
    x_sum,
    z_in,
    final,
    back_send,
    back_recv,
    ring_send,
    ring_recv,
    core_send,
    core_recv,
    y_send,
    y_recv,
    x_send,
    x_recv,
    z_send,
    z_recv,
    dp_send,
    dp_recv,
):
    dp, x, z = place()
    graph = x * ZN + z
    y, core = dp // 2, dp % 2
    partner = (y * 2 + (1 - core), graph)
    x_peers = [None] + [(dp, ((x + k) % XN) * ZN + z) for k in range(1, XN)]
    z_peers = [None] + [(dp, x * ZN + (z + k) % ZN) for k in range(1, ZN)]
    y_peers = [None] + [(((y + k) % YN) * 2 + core, graph) for k in range(1, YN)]
    dp_peers = [None] + [((dp + k) % 8, graph) for k in range(1, 8)]
    enter(x_peers[1:] + z_peers[1:] + dp_peers[1:])
    up, down = z_peers[1], z_peers[ZN - 1]
    sent = []

    def start(src, dst, send, recv, device):
        copy = remote(src, dst, send, recv, device)
        copy.start()
        sent.append(copy)
        return copy

    other = (1 - core) * 4
    mine = core * 4
    core_copies = []
    for j in range(YN):
        tile = (y + YN - j) % YN if False else j
        core_copies.append(
            start(
                grads_ref.at[pl.ds(other, 4), :, tile * 128 : (tile + 1) * 128],
                core_in.at[tile],
                core_send.at[tile],
                core_recv.at[tile],
                partner,
            )
        )
    row_copies = {}
    for j in REDUCE_ORDER:
        target = (z + REDUCE_OFFSET[j] + ZN) % ZN
        rows_in[j, x] = back_ref[x * ZN + target]
        row_copies[j] = [
            start(
                back_ref.at[((x + k) % XN) * ZN + target],
                rows_in.at[j, x],
                back_send.at[j, k - 1],
                back_recv.at[j, k - 1],
                x_peers[k],
            )
            for k in range(1, XN)
        ]
    for j in range(YN):
        core_copies[j].wait_recv()
        pair[j] = (
            grads_ref[pl.ds(mine, 4), :, j * 128 : (j + 1) * 128].astype(F32) + core_in[j].astype(F32)
        ).astype(BF16)
    y_copies = [
        start(pair.at[(y + k) % YN], y_in.at[k - 1], y_send.at[k - 1], y_recv.at[k - 1], y_peers[k])
        for k in (2, 1, 3)
    ]

    ring_copies = {}
    for j in REDUCE_ORDER:
        target = (z + REDUCE_OFFSET[j] + ZN) % ZN
        for copy in row_copies[j]:
            copy.wait_recv()
        total = nn(onehot_rows(ND, list_ref[pl.ds(target, 1), :]), rows_in[j].reshape(ND, D))
        if j in (3, 2, 1, 6, 5):
            ring_copies[j + 1].wait_recv()
            total = total + ring_in[j + 1].astype(F32)
        if j == 0:
            ring_copies[1].wait_recv()
            ring_copies[5].wait_recv()
            total = total + ring_in[1].astype(F32) + ring_in[5].astype(F32)
            node_grad_ref[...] = (node_part_ref[...] + nt(total.astype(BF16), weight_ref[1])).astype(BF16)
        else:
            ring_out[j] = total.astype(BF16)
            ring_copies[j] = start(
                ring_out.at[j], ring_in.at[j], ring_send.at[j], ring_recv.at[j], up if j < 5 else down
            )

    for copy in y_copies:
        copy.wait_recv()
    y_sum[...] = (
        pair[y].astype(F32) + y_in[0].astype(F32) + y_in[1].astype(F32) + y_in[2].astype(F32)
    ).astype(BF16)
    x_copies = [
        start(
            y_sum.at[:, pl.ds(pl.multiple_of(((x + k) % XN) * 128, 128), 128), :],
            x_in.at[k - 1],
            x_send.at[k - 1],
            x_recv.at[k - 1],
            x_peers[k],
        )
        for k in (2, 1, 3)
    ]
    for copy in x_copies:
        copy.wait_recv()
    x_sum[...] = (
        y_sum[:, pl.ds(pl.multiple_of(x * 128, 128), 128), :].astype(F32)
        + x_in[0].astype(F32)
        + x_in[1].astype(F32)
        + x_in[2].astype(F32)
    ).astype(BF16)
    z_copies = [
        start(
            x_sum.at[:, pl.ds(pl.multiple_of(((z + k) % ZN) * 16, 16), 16), :],
            z_in.at[k - 1],
            z_send.at[k - 1],
            z_recv.at[k - 1],
            z_peers[k],
        )
        for k in (4, 3, 5, 2, 6, 1, 7)
    ]
    for copy in z_copies:
        copy.wait_recv()
    total = x_sum[:, pl.ds(pl.multiple_of(z * 16, 16), 16), :].astype(F32)
    for k in range(ZN - 1):
        total = total + z_in[k].astype(F32)
    final[dp] = total
    dp_copies = [
        start(final.at[dp], final.at[dp], dp_send.at[k - 1], dp_recv.at[k - 1], dp_peers[k]) for k in range(1, 8)
    ]
    for copy in dp_copies:
        copy.wait_recv()
    for j in range(YN):
        lanes = slice(j * 128, (j + 1) * 128)
        for m in range(3):
            edge_first_ref[m, :, lanes] = final[2 * j, m]
        edge_second_ref[:, lanes] = final[2 * j, 3]
        for m in range(2):
            node_first_ref[m, :, lanes] = final[2 * j + 1, m]
        node_second_ref[:, lanes] = final[2 * j + 1, 2]
    columns_ref[...] = final[1, 3]
    for copy in sent:
        copy.wait_send()


def reduce(back, lists, grads, node_part, weight):
    vmem = pl.BlockSpec(memory_space=pltpu.VMEM)
    dma = pltpu.SemaphoreType.DMA
    return pl.pallas_call(
        reduce_kernel,
        out_shape=(
            jax.ShapeDtypeStruct((ND, D), BF16),
            jax.ShapeDtypeStruct((3, 16, D), F32),
            jax.ShapeDtypeStruct((16, D), F32),
            jax.ShapeDtypeStruct((2, 16, D), F32),
            jax.ShapeDtypeStruct((16, D), F32),
            jax.ShapeDtypeStruct((16, 128), F32),
        ),
        in_specs=[vmem] * 5,
        out_specs=(vmem,) * 6,
        scratch_shapes=[
            pltpu.VMEM((ZN, XN, SLOTS, D), BF16),
            pltpu.VMEM((ZN, ND, D), BF16),
            pltpu.VMEM((ZN, ND, D), BF16),
            pltpu.VMEM((YN, 4, D, 128), BF16),
            pltpu.VMEM((YN, 4, D, 128), BF16),
            pltpu.VMEM((YN - 1, 4, D, 128), BF16),
            pltpu.VMEM((4, D, 128), BF16),
            pltpu.VMEM((XN - 1, 4, 128, 128), BF16),
            pltpu.VMEM((4, 128, 128), BF16),
            pltpu.VMEM((ZN - 1, 4, 16, 128), BF16),
            pltpu.VMEM((8, 4, 16, 128), F32),
            dma((ZN, XN - 1)),
            dma((ZN, XN - 1)),
            dma((ZN,)),
            dma((ZN,)),
            dma((YN,)),
            dma((YN,)),
            dma((YN - 1,)),
            dma((YN - 1,)),
            dma((XN - 1,)),
            dma((XN - 1,)),
            dma((ZN - 1,)),
            dma((ZN - 1,)),
            dma((7,)),
            dma((7,)),
        ],
        compiler_params=pltpu.CompilerParams(
            collective_id=1, has_side_effects=True, vmem_limit_bytes=VMEM_LIMIT
        ),
        name="reduce",
    )(back, lists, grads, node_part, weight)


def body(
    node_latents,
    edge_latents,
    senders,
    receivers,
    block_counts,
    edge_first,
    edge_second,
    node_first,
    node_second,
    vectors,
    node_cotangent,
    edge_cotangent,
):
    node = node_latents[0]
    buf, slot, lists = exchange(node, senders)
    new_nodes, new_edges, edge_grad, node_part, back, grads = dense(
        block_counts,
        node,
        edge_latents.reshape(EDGES, D),
        buf.reshape(EDGES, D),
        slot,
        receivers,
        edge_first,
        edge_second,
        node_first,
        node_second,
        vectors,
        node_cotangent[0],
        edge_cotangent.reshape(EDGES, D),
    )
    node_grad, grad_ef, grad_es, grad_nf, grad_ns, columns = reduce(
        back.reshape(GN, SLOTS, D), lists, grads, node_part, edge_first
    )
    shape = edge_latents.shape
    return (
        new_nodes[None],
        new_edges.reshape(shape),
        node_grad[None],
        edge_grad.reshape(shape),
        grad_ef,
        grad_es,
        grad_nf,
        grad_ns,
        columns[:, 0:4].T,
    )


def solution(mesh):
    return jax.shard_map(
        body,
        mesh=mesh,
        in_specs=(
            P("dp", "graph", None),
            P("dp", "graph", None, None),
            P("graph", None),
            P("graph", None),
            P("graph"),
            P(),
            P(),
            P(),
            P(),
            P(),
            P("dp", "graph", None),
            P("dp", "graph", None, None),
        ),
        out_specs=(
            P("dp", "graph", None),
            P("dp", "graph", None, None),
            P("dp", "graph", None),
            P("dp", "graph", None, None),
            P(None, "graph", None),
            P("graph", None),
            P(None, "graph", None),
            P("graph", None),
            P(None, "graph"),
        ),
        check_vma=False,
    )
```

time: 860 us -> 116 us (0.13)
  waiting for transfers between devices: 726 us -> 0 us
  Pallas kernels: 0 us -> 106 us
  matrix products: 36.1 us -> 0 us
  other arithmetic: 33.9 us -> 0 us
  blocking collectives: 17.9 us -> 0 us
  local copies, waits for them, and re-layouts: 26.5 us -> 8.68 us
  between operations: 14.8 us -> 1.31 us
    reduce_scatter x2 -> x0, waiting for transfers between devices: 431 us -> none  [the longest x1 216 us: body(): lax.psum_scatter(dense_send.astype(jnp.bfloat16), 'graph', scatter_dimens...]
    unnamed x6 -> x0, waiting for transfers between devices: 170 us -> none
    pallas_call x0 -> x3, Pallas kernels: none -> 106 us  [the longest x1 57.8 us: reduce(): pl.pallas_call(reduce_kernel, out_shape=(jax.ShapeDtypeStruct((ND, D), BF...]
    all_gather x1 -> x0, waiting for transfers between devices: 76.3 us -> none  [body(): all_nodes = lax.all_gather(node_latents, 'graph', axis=1, tiled=True)[0]]
    psum x1 -> x0, waiting for transfers between devices: 49.1 us -> none  [body(): lax.psum(matrices.astype(jnp.bfloat16), 'dp').astype(jnp.float32)]
    dot_general x23 -> x0, matrix products: 36.1 us -> none  [the longest x6 11.2 us: product_back(): lax.dot_general(left, right, (((1,), (1,)), ((), ())), preferred_element_...]
    psum x1 -> x0, blocking collectives: 17.9 us -> none  [body(): lax.psum(columns.astype(jnp.bfloat16), 'dp').astype(jnp.float32)]
    scatter-add x2 -> x0, other arithmetic: 17.7 us -> none  [the longest x1 11 us: body(): jax.ops.segment_sum(product_back(edge_dpre, edge_first[1]), send_index, n...]
  transfers between devices with their start and end apart: 5 -> 0, of which waited for: 5 -> 0; matrix products, arithmetic and copies ran while one was open for 5% -> 0% of each run, Pallas kernels for 0% -> 0%
where the time goes in v1:
time: 116 us
  Pallas kernels  106 us (91%)
  local copies, waits for them, and re-layouts  8.68 us (7%)
  between operations  1.31 us (1%)
    pallas_call x1, Pallas kernels, reduce(): pl.pallas_call(reduce_kernel, out_shape=(jax.ShapeDtypeStruct((ND, D), BF...  57.8 us
    pallas_call x1, Pallas kernels, exchange(): pl.pallas_call(exchange_kernel, out_shape=(jax.ShapeDtypeStruct((GN, SLOT...  29.5 us
    pallas_call x1, Pallas kernels, dense(): pl.pallas_call(dense_kernel, out_shape=(jax.ShapeDtypeStruct((ND, D), BF1...  18.6 us
    unnamed x6, local copies, waits for them, and re-layouts  7.98 us

profile of v1, /device:TPU:1, one launch (start us, length us, event | category | flops | bytes accessed | tf_op | source)
XLA Modules:
  0.0 115.9 jit_solution(18032108177583243704)
XLA Ops:
  1.3 29.5 %exchange.1 = (bf16[32,32,512]{2,1,0:T(8,128)(2,1)}, s32[8,128]{1,0:T(8,128)}, s32[8,128]{1,0:T(8,128)}) custom-call(bf16[128,512]{1,0:T(8,128)(2,1)} %bitcast.16, s32[8,128]{1,0:T(8,128)} %senders_ref.1), custom_call_target="tpu_custom_call" | custom-call | tf_op jit(solution)/shard_map/exchange/pallas_call | solution.py:156
  30.8 18.6 %dense.1 = (bf16[128,512]{1,0:T(8,128)(2,1)}, bf16[1024,512]{1,0:T(8,128)(2,1)}, bf16[1024,512]{1,0:T(8,128)(2,1)}, f32[128,512]{1,0:T(8,128)}, bf16[1024,512]{1,0:T(8,128)(2,1)}, /*index=5*/bf16[8,512,512]{2,1,0:T(8,128)(2,1)}) custom-call(s32[1]{0:T(128)S(6)} %copy.27.counts_ref, bf16[128,512]{1,0:T(8,128)(2,1)} %bitcast.17, bf16[1024,512]{1,0:T(8,128)(2,1)} %bitcast.12, ...), custom_call_target="tpu_custom_call" | custom-call | tf_op jit(solution)/shard_map/dense/pallas_call | solution.py:323
  49.4 57.8 %reduce.1 = (bf16[128,512]{1,0:T(8,128)(2,1)}, f32[3,16,512]{2,1,0:T(8,128)}, f32[16,512]{1,0:T(8,128)}, f32[2,16,512]{2,1,0:T(8,128)}, f32[16,512]{1,0:T(8,128)}, /*index=5*/f32[16,128]{1,0:T(8,128)}) custom-call(bf16[32,32,512]{2,1,0:T(8,128)(2,1)} %bitcast.15, s32[8,128]{1,0:T(8,128)} %get-tuple-element.29.list_ref, ...), custom_call_target="tpu_custom_call" | custom-call | tf_op jit(solution)/shard_map/reduce/pallas_call | solution.py:528
  107.2 0.7 slice_bitcast_fusion
  107.9 0.7 copy.21
  108.6 1.6 %copy.28 = bf16[1,128,512]{2,1,0:T(8,128)(2,1)} copy(bf16[1,128,512]{2,1,0:T(8,128)(2,1)} %bitcast.19) | data formatting | bytes 262144
  110.2 1.5 %copy.29 = f32[3,16,512]{2,1,0:T(8,128)} copy(f32[3,16,512]{2,1,0:T(8,128)} %get-tuple-element.61) | data formatting | bytes 196608
  111.7 1.4 %copy.30 = f32[16,512]{1,0:T(8,128)} copy(f32[16,512]{1,0:T(8,128)} %get-tuple-element.62) | data formatting | bytes 65536
  113.1 1.5 %copy.31 = f32[2,16,512]{2,1,0:T(8,128)} copy(f32[2,16,512]{2,1,0:T(8,128)} %get-tuple-element.63) | data formatting | bytes 131072
  114.5 1.4 %copy.32 = f32[16,512]{1,0:T(8,128)} copy(f32[16,512]{1,0:T(8,128)} %get-tuple-element.64) | data formatting | bytes 65536

commit v2 on v0

v2 whole, which is shorter than its diff:
```python
from types import SimpleNamespace

import jax
import jax.numpy as jnp
from jax import lax
from jax.experimental import pallas as pl
from jax.experimental.pallas import tpu as pltpu
from jax.sharding import PartitionSpec as P

EPSILON = 1e-05
MESH = pl.DeviceIdType.MESH
F32 = jnp.float32
BF16 = jnp.bfloat16

XN, ZN, YN = 4, 8, 4
GN = XN * ZN
ND = 128
D = 512
EDGES = 1024
SLOTS = 32
BM = 256
NB = EDGES // BM
VMEM_LIMIT = 56 * 1024 * 1024

RING_ORDER = (0, 1, 5, 2, 6, 3, 7, 4)
RING_OFFSET = (0, -1, -2, -3, -4, 1, 2, 3)


def nn(left, right):
    return jnp.dot(left, right, preferred_element_type=F32)


def nt(left, right):
    return lax.dot_general(left, right, (((1,), (1,)), ((), ())), preferred_element_type=F32)


def tn(left, right):
    return lax.dot_general(left, right, (((0,), (0,)), ((), ())), preferred_element_type=F32)


def place():
    dp = lax.axis_index("dp")
    graph = lax.axis_index("graph")
    return dp, graph // ZN, graph % ZN


def remote(src, dst, send, recv, device):
    return pltpu.make_async_remote_copy(
        src_ref=src, dst_ref=dst, send_sem=send, recv_sem=recv, device_id=device, device_id_type=MESH
    )


def enter(devices):
    barrier = pltpu.get_barrier_semaphore()
    for device in devices:
        pl.semaphore_signal(barrier, inc=1, device_id=device, device_id_type=MESH)
    pl.semaphore_wait(barrier, len(devices))


def onehot_rows(count, row):
    index = lax.broadcasted_iota(jnp.int32, (count, row.shape[1]), 0)
    return jnp.where(index == row, 1.0, 0.0).astype(BF16)


def normalize(values):
    average = jnp.mean(values, -1, keepdims=True)
    centered = values - average
    inverse = lax.rsqrt(jnp.mean(centered * centered, -1, keepdims=True) + EPSILON)
    return centered * inverse, inverse


def norm_backward(upstream, normed, inverse, scales):
    scaled = upstream * scales
    return inverse * (
        scaled
        - jnp.mean(scaled, -1, keepdims=True)
        - normed * jnp.mean(scaled * normed, -1, keepdims=True)
    )


def sigmoid(values):
    return 0.5 + 0.5 * jnp.tanh(0.5 * values)


REDUCE_ORDER = (4, 7, 3, 6, 2, 5, 1, 0)
REDUCE_OFFSET = (0, 1, 2, 3, 4, -1, -2, -3)
PARTS = 2
CHUNK = 256


def hot_columns(column, count):
    index = lax.broadcasted_iota(jnp.int32, (column.shape[0], count), 1)
    return jnp.where(index == column, 1.0, 0.0).astype(BF16)


def columns_of(rows):
    padded = jnp.concatenate([rows.astype(F32), jnp.zeros((128 - rows.shape[0], 128), F32)], axis=0)
    return padded.T.astype(jnp.int32)


def layer_kernel(
    counts_ref,
    node_ref,
    senders_ref,
    recv_ref,
    vectors_ref,
    edge_hbm,
    edge_first_hbm,
    edge_second_hbm,
    node_first_hbm,
    node_second_hbm,
    node_cot_hbm,
    edge_cot_hbm,
    new_nodes_hbm,
    new_edges_hbm,
    edge_grad_hbm,
    node_grad_ref,
    final_edge,
    final_node,
    sums_ref,
    held,
):
    s = SimpleNamespace(**held)
    dp, x, z = place()
    graph = x * ZN + z
    y, core = dp // 2, dp % 2
    partner = (y * 2 + (1 - core), graph)
    x_peers = [None] + [(dp, ((x + k) % XN) * ZN + z) for k in range(1, XN)]
    z_peers = [None] + [(dp, x * ZN + (z + k) % ZN) for k in range(1, ZN)]
    y_peers = [None] + [(((y + k) % YN) * 2 + core, graph) for k in range(1, YN)]
    dp_peers = [None] + [((dp + k) % 8, graph) for k in range(1, 8)]
    up, down = z_peers[1], z_peers[ZN - 1]

    loads = {}
    for index, (hbm, ref) in enumerate(
        (
            (edge_first_hbm, s.edge_first),
            (edge_hbm, s.edges),
            (edge_second_hbm, s.edge_second),
            (node_first_hbm, s.node_first),
            (node_second_hbm, s.node_second),
            (node_cot_hbm, s.node_cot),
            (edge_cot_hbm, s.edge_cot),
        )
    ):
        loads[index] = pltpu.make_async_copy(hbm, ref, s.load_sem.at[index])
        loads[index].start()
    edges, edge_first, edge_second = s.edges, s.edge_first, s.edge_second
    node_first, node_second = s.node_first, s.node_second
    edge_cot, node_cot = s.edge_cot, s.node_cot

    enter(x_peers[1:] + z_peers[1:] + dp_peers[1:])
    sent = []

    def start(src, dst, sems, index, device):
        copy = remote(src, dst, sems[0].at[index], sems[1].at[index], device)
        copy.start()
        sent.append(copy)
        return copy

    ring, buf = s.ring, s.buf
    rows_of = ND // PARTS

    def hop(src, slot, device, part):
        piece = pl.ds(part * rows_of, rows_of)
        return start(src.at[piece], ring.at[slot, piece], s.hop_sems, (slot, part), device)

    hops = {}
    for part in range(PARTS):
        hops[1, part] = hop(node_ref, 1, up, part)
        hops[5, part] = hop(node_ref, 5, down, part)

    senders = senders_ref[...]
    owners = senders // ND
    local = (senders % ND).astype(F32)
    earlier = jnp.where(
        lax.broadcasted_iota(jnp.int32, (ND, ND), 0) < lax.broadcasted_iota(jnp.int32, (ND, ND), 1), 1.0, 0.0
    ).astype(BF16)
    base = jnp.zeros((GN, 1), F32)
    table = jnp.zeros((GN, ND), F32)
    lane = lax.broadcasted_iota(jnp.int32, (ND, ND), 0)
    group = lax.broadcasted_iota(jnp.int32, (GN, ND), 0)
    slot_rows = []
    for b in range(EDGES // ND):
        owner = owners[b : b + 1, :]
        mine = jnp.where(group == owner, 1.0, 0.0)
        before = nn(mine.astype(BF16), earlier) + base
        rank = jnp.sum(mine * before, axis=0, keepdims=True).astype(jnp.int32)
        base = base + jnp.sum(mine, axis=1, keepdims=True)
        slot_rows.append(owner * SLOTS + rank)
        column = jnp.where(lane == rank + SLOTS * x, 1.0, 0.0).astype(BF16)
        table = table + nt((mine * local[b : b + 1, :]).astype(BF16), column)
    lists_own, lists_in, lists = s.lists_own, s.lists_in, s.lists
    lists_own[...] = table.reshape(XN, ZN, ND)
    list_copies = [
        start(lists_own.at[(x + k) % XN], lists_in.at[k - 1], s.list_sems, k - 1, x_peers[k]) for k in range(1, XN)
    ]
    slot_columns = columns_of(jnp.concatenate(slot_rows, axis=0))
    recv = recv_ref[...] - graph * ND
    recv_columns = columns_of(recv)
    perm, perm_back, hot, hot_back, slope = s.perm, s.perm_back, s.hot, s.hot_back, s.slope
    h = node_ref[...]

    def fill(step):
        if step == 0:
            loads[0].wait()
            s.h_recv[...] = nn(h, edge_first[2]).astype(BF16)
        elif step == 1:
            loads[1].wait()
        if 1 <= step <= NB:
            i = step - 1
            rows = slice(i * BM, (i + 1) * BM)
            for b in range(i * BM // 128, (i + 1) * BM // 128):
                block = slice(b * 128, (b + 1) * 128)
                perm[block, :] = hot_columns(slot_columns[:, b : b + 1], EDGES)
                perm_back[:, block] = onehot_rows(EDGES, slot_rows[b])
                hot[block, :] = hot_columns(recv_columns[:, b : b + 1], ND)
                hot_back[:, block] = onehot_rows(ND, recv[b : b + 1, :])
            slope[rows, :] = (
                nn(edges[rows, :], edge_first[0]) + nn(hot[rows, :], s.h_recv[...]) + vectors_ref[0:1, :]
            )

    stage = s.stage
    x_copies = []

    def forward(slot, part):
        hops[slot, part].wait_recv()
        if slot in (1, 2, 3):
            hops[slot + 1, part] = hop(ring.at[slot], slot + 1, up, part)
        elif slot in (5, 6):
            hops[slot + 1, part] = hop(ring.at[slot], slot + 1, down, part)

    def relay(slot):
        source = (z + RING_OFFSET[slot] + ZN) % ZN
        chosen = onehot_rows(ND, lists[pl.ds(source, 1), :])
        stage[slot] = tn(chosen, ring[slot] if slot else h).astype(BF16).reshape(XN, SLOTS, D)
        for k in range(1, XN):
            x_copies.append(
                start(stage.at[slot, (x + k) % XN], buf.at[x * ZN + source], s.away_sems, (slot, k - 1), x_peers[k])
            )
        buf[x * ZN + source] = stage[slot, x]

    fill(0)
    for copy in list_copies:
        copy.wait_recv()
    lists[...] = (lists_own[x] + lists_in[0] + lists_in[1] + lists_in[2]).astype(jnp.int32)
    for step, slots in enumerate(((1, 5), (2, 6), (3, 7), (4,)), 1):
        for part in range(PARTS):
            for slot in slots:
                forward(slot, part)
        for slot in slots if step > 1 else (0,) + slots:
            relay(slot)
        fill(step)
    for index in range(2, 7):
        loads[index].wait()
    for copy in x_copies:
        copy.wait_recv()

    live_rows = counts_ref[0] * 128
    act, normed, inverse, new_edges = s.act, s.normed, s.inverse, s.new_edges
    aggregate = jnp.zeros((ND, D), F32)
    for i in range(NB):
        rows = slice(i * BM, (i + 1) * BM)
        sent_rows = nn(perm[rows, :], buf[...].reshape(EDGES, D)).astype(BF16)
        pre = slope[rows, :] + nn(sent_rows, edge_first[1])
        gate = sigmoid(pre)
        act_b = (pre * gate).astype(BF16)
        act[rows, :] = act_b
        slope[rows, :] = gate * (1.0 + pre * (1.0 - gate))
        hat, inv = normalize(nn(act_b, edge_second[...]))
        normed[rows, :] = hat
        inverse[rows, :] = inv
        live = lax.broadcasted_iota(jnp.int32, (BM, 1), 0) + i * BM < live_rows
        message = jnp.where(live, hat * vectors_ref[2:3, :], 0.0).astype(BF16)
        new_edges[rows, :] = (edges[rows, :].astype(F32) + message.astype(F32)).astype(BF16)
        aggregate = aggregate + nn(hot_back[:, rows], message)
    store_edges = pltpu.make_async_copy(new_edges, new_edges_hbm, s.store_sem.at[0])
    store_edges.start()
    aggregate = aggregate.astype(BF16)

    grads = s.grads
    node_pre = nn(h, node_first[0]) + nn(aggregate, node_first[1]) + vectors_ref[1:2, :]
    node_gate = sigmoid(node_pre)
    node_act = (node_pre * node_gate).astype(BF16)
    node_hat, node_inv = normalize(nn(node_act, node_second[...]))
    s.new_nodes[...] = (h.astype(F32) + node_hat * vectors_ref[3:4, :]).astype(BF16)
    store_nodes = pltpu.make_async_copy(s.new_nodes, new_nodes_hbm, s.store_sem.at[1])
    store_nodes.start()
    upstream = node_cot[...].astype(F32)
    node_dz = norm_backward(upstream, node_hat, node_inv, vectors_ref[3:4, :]).astype(BF16)
    node_dpre = (
        nt(node_dz, node_second[...]) * (node_gate * (1.0 + node_pre * (1.0 - node_gate)))
    ).astype(BF16)
    aggregate_cot = nt(node_dpre, node_first[1]).astype(BF16)
    col_node = jnp.sum(node_dpre.astype(F32), 0, keepdims=True)
    col_node_scale = jnp.sum(upstream * node_hat, 0, keepdims=True)
    grads[4] = tn(h, node_dpre).astype(BF16)
    grads[5] = tn(aggregate, node_dpre).astype(BF16)
    grads[6] = tn(node_act, node_dz).astype(BF16)
    s.node_part[...] = upstream + nt(node_dpre, node_first[0])

    def make(src, dst, sems, index, device):
        return remote(src, dst, sems[0].at[index], sems[1].at[index], device)

    def row_chunk(index):
        return pl.ds(pl.multiple_of(index * 128, 128), 128)

    class Share:
        def __init__(self, owner, first, count, held, final):
            t = SimpleNamespace(**held)
            self.owner, self.first, self.count, self.final = owner, first, count, final
            self.core_in, self.pair = t.core_in, t.pair
            self.a_in, self.a_sum = t.a_in, t.a_sum
            self.b_in, self.b_sum, self.z_in = t.b_in, t.b_sum, t.z_in
            columns_first = owner == 0
            if columns_first:
                self.a_place, self.b_place, a_peers, b_peers = y, x, y_peers, x_peers
                self.cuts = [(slice(None), slice(j * 128, (j + 1) * 128)) for j in range(4)]
            else:
                self.a_place, self.b_place, a_peers, b_peers = x, y, x_peers, y_peers
                self.cuts = [(slice(j * 128, (j + 1) * 128), slice(None)) for j in range(4)]

            def b_cut(k):
                piece = row_chunk((self.b_place + k) % 4)
                return (slice(None), piece, slice(None)) if columns_first else (slice(None), slice(None), piece)

            self.b_own = b_cut(0)
            self.core_copies = [
                make(grads.at[first + m], self.core_in.at[m], t.core_sems, m, partner) for m in range(count)
            ]
            self.a_copies = [
                [
                    make(self.pair.at[(self.a_place + k) % 4, m], self.a_in.at[k - 1, m], t.a_sems, (k - 1, m), a_peers[k])
                    for k in (2, 1, 3)
                ]
                for m in range(count)
            ]
            self.b_copies = [
                make(self.a_sum.at[b_cut(k)], self.b_in.at[k - 1], t.b_sems, k - 1, b_peers[k]) for k in (2, 1, 3)
            ]
            self.z_copies = [
                make(
                    self.b_sum.at[:, pl.ds(pl.multiple_of(((z + k) % ZN) * 16, 16), 16), :],
                    self.z_in.at[k - 1],
                    t.z_sems,
                    k - 1,
                    z_peers[k],
                )
                for k in (4, 3, 5, 2, 6, 1, 7)
            ]
            self.dp_copies = [
                remote(final.at[y], final.at[y], t.dp_sems[0].at[k - 1], t.dp_sems[1].at[y], dp_peers[k])
                for k in range(1, 8)
            ]
            self.dp_in = [
                remote(
                    final.at[(y + k) % YN],
                    final.at[(y + k) % YN],
                    t.dp_sems[0].at[0],
                    t.dp_sems[1].at[(y + k) % YN],
                    dp_peers[1],
                )
                for k in range(YN)
            ]

        def give(self, m):
            @pl.when(core != self.owner)
            def _():
                self.core_copies[m].start()

        def across_a(self, m):
            @pl.when(core == self.owner)
            def _():
                self.core_copies[m].wait_recv()
                for j, (rows, lanes) in enumerate(self.cuts):
                    self.pair[j, m] = (
                        grads[self.first + m, rows, lanes].astype(F32) + self.core_in[m, rows, lanes].astype(F32)
                    ).astype(BF16)
                for copy in self.a_copies[m]:
                    copy.start()

        def across_b(self):
            @pl.when(core == self.owner)
            def _():
                for m in range(self.count):
                    for copy in self.a_copies[m]:
                        copy.wait_recv()
                    self.a_sum[m] = (
                        self.pair[self.a_place, m].astype(F32)
                        + self.a_in[0, m].astype(F32)
                        + self.a_in[1, m].astype(F32)
                        + self.a_in[2, m].astype(F32)
                    ).astype(BF16)
                for copy in self.b_copies:
                    copy.start()

        def across_z(self):
            @pl.when(core == self.owner)
            def _():
                for copy in self.b_copies:
                    copy.wait_recv()
                self.b_sum[...] = (
                    self.a_sum[self.b_own].astype(F32)
                    + self.b_in[0].astype(F32)
                    + self.b_in[1].astype(F32)
                    + self.b_in[2].astype(F32)
                ).astype(BF16)
                for copy in self.z_copies:
                    copy.start()

        def across_dp(self):
            @pl.when(core == self.owner)
            def _():
                for copy in self.z_copies:
                    copy.wait_recv()
                total = self.b_sum[:, pl.ds(pl.multiple_of(z * 16, 16), 16), :].astype(F32)
                for k in range(ZN - 1):
                    total = total + self.z_in[k].astype(F32)
                self.final[y] = total.astype(BF16)
                for copy in self.dp_copies:
                    copy.start()

        def finish(self):
            for k in range(YN):
                if k:
                    self.dp_in[k].wait_recv()
                else:

                    @pl.when(core != self.owner)
                    def _():
                        self.dp_in[0].wait_recv()

        def drain(self):
            @pl.when(core != self.owner)
            def _():
                for copy in self.core_copies:
                    copy.wait_send()

            @pl.when(core == self.owner)
            def _():
                for copies in self.a_copies:
                    for copy in copies:
                        copy.wait_send()
                for copy in self.b_copies + self.z_copies + self.dp_copies:
                    copy.wait_send()

    node_share = Share(1, 4, 3, s.node_share, final_node)
    edge_share = Share(0, 0, 4, s.edge_share, final_edge)
    for m in range(3):
        node_share.give(m)

    dz, dpre = s.dz, s.dpre
    col_scale = jnp.zeros((1, D), F32)
    for i in range(NB):
        rows = slice(i * BM, (i + 1) * BM)
        live = lax.broadcasted_iota(jnp.int32, (BM, 1), 0) + i * BM < live_rows
        message_cot = jnp.where(live, edge_cot[rows, :].astype(F32) + nn(hot[rows, :], aggregate_cot), 0.0)
        hat = normed[rows, :]
        col_scale = col_scale + jnp.sum(message_cot * hat, 0, keepdims=True)
        dz[rows, :] = norm_backward(message_cot, hat, inverse[rows, :], vectors_ref[2:3, :]).astype(BF16)
        if i == NB // 2 - 1:
            for m in range(3):
                node_share.across_a(m)
    grads[3] = tn(act[...], dz[...]).astype(BF16)
    edge_share.give(3)
    col_edge = jnp.zeros((1, D), F32)
    received = jnp.zeros((ND, D), F32)
    for i in range(NB):
        rows = slice(i * BM, (i + 1) * BM)
        dpre_b = (nt(dz[rows, :], edge_second[...]) * slope[rows, :]).astype(BF16)
        dpre[rows, :] = dpre_b
        col_edge = col_edge + jnp.sum(dpre_b.astype(F32), 0, keepdims=True)
        received = received + nn(hot_back[:, rows], dpre_b)
    received = received.astype(BF16)
    edge_share.across_a(3)
    grads[2] = tn(h, received).astype(BF16)
    edge_share.give(2)
    grads[0] = tn(edges[...], dpre[...]).astype(BF16)
    edge_share.give(0)
    back = s.back
    back[...] = nn(perm_back[...], dpre[...]).astype(BF16).reshape(GN, SLOTS, D)
    rows_in = s.rows_in
    row_copies = {}
    for j in REDUCE_ORDER:
        target = (z + REDUCE_OFFSET[j] + ZN) % ZN
        row_copies[j] = [
            start(back.at[((x + k) % XN) * ZN + target], rows_in.at[j, x], s.row_sems, (j, k - 1), x_peers[k])
            for k in range(1, XN)
        ]
    edge_share.across_a(2)
    grads[1] = tn(buf[...].reshape(EDGES, D), back[...].reshape(EDGES, D)).astype(BF16)
    edge_share.give(1)
    edge_share.across_a(0)

    sums = s.sums
    sums[0] = jnp.concatenate([col_edge, col_node, col_scale, col_node_scale, jnp.zeros((4, D), F32)], axis=0)
    dp_sums = [start(sums.at[0], s.dp_sums.at[k - 1], s.sdp_sems, k - 1, dp_peers[k]) for k in range(1, 8)]
    for j in REDUCE_ORDER:
        target = (z + REDUCE_OFFSET[j] + ZN) % ZN
        rows_in[j, x] = back[x * ZN + target]
    edge_share.across_a(1)
    node_share.across_b()

    ring_out, ring_in = s.ring_out, s.ring_in
    ring_copies = {}

    def ring_step(j):
        target = (z + REDUCE_OFFSET[j] + ZN) % ZN
        for copy in row_copies[j]:
            copy.wait_recv()
        total = nn(onehot_rows(ND, lists[pl.ds(target, 1), :]), rows_in[j].reshape(ND, D))
        if j:
            for part in range(PARTS):
                piece = slice(part * rows_of, (part + 1) * rows_of)
                partial = total[piece]
                if j in (3, 2, 1, 6, 5):
                    ring_copies[j + 1, part].wait_recv()
                    partial = partial + ring_in[j + 1, piece].astype(F32)
                ring_out[j, piece] = partial.astype(BF16)
                ring_copies[j, part] = start(
                    ring_out.at[j, piece], ring_in.at[j, piece], s.back_sems, (j, part), up if j < 5 else down
                )
            return
        for part in range(PARTS):
            ring_copies[1, part].wait_recv()
            ring_copies[5, part].wait_recv()
        total = total + ring_in[1].astype(F32) + ring_in[5].astype(F32)
        node_grad_ref[...] = (
            s.node_part[...] + nt(total.astype(BF16), edge_first[1]) + nt(received, edge_first[2])
        ).astype(BF16)

    def sum_step(parts, source, index):
        total = sums[source]
        for k in range(parts.shape[0]):
            total = total + parts[k]
        sums[index] = total

    edge_grad = s.edge_grad
    for i in range(NB):
        rows = slice(i * BM, (i + 1) * BM)
        edge_grad[rows, :] = (edge_cot[rows, :].astype(F32) + nt(dpre[rows, :], edge_first[0])).astype(BF16)
        if i % 2:
            ring_step(REDUCE_ORDER[i // 2])
    store_grad = pltpu.make_async_copy(edge_grad, edge_grad_hbm, s.store_sem.at[2])
    store_grad.start()
    for copy in dp_sums:
        copy.wait_recv()
    sum_step(s.dp_sums, 0, 1)
    x_sums = [start(sums.at[1], s.x_sums.at[k - 1], s.sx_sems, k - 1, x_peers[k]) for k in range(1, XN)]
    ring_step(3)
    ring_step(6)
    node_share.across_z()
    ring_step(2)
    ring_step(5)
    edge_share.across_b()
    for copy in x_sums:
        copy.wait_recv()
    sum_step(s.x_sums, 1, 2)
    z_sums = [start(sums.at[2], s.z_sums.at[k - 1], s.sz_sems, k - 1, z_peers[k]) for k in range(1, ZN)]
    ring_step(1)
    node_share.across_dp()
    edge_share.across_z()
    ring_step(0)
    for copy in z_sums:
        copy.wait_recv()
    sum_step(s.z_sums, 2, 3)
    sums_ref[...] = sums[3]
    node_share.finish()
    edge_share.across_dp()
    store_edges.wait()
    store_nodes.wait()
    store_grad.wait()
    for copy in sent:
        copy.wait_send()
    edge_share.finish()
    node_share.drain()
    edge_share.drain()


def scratch():
    v, dma = pltpu.VMEM, pltpu.SemaphoreType.DMA

    def pair(*size):
        return dma(size), dma(size)

    def share(count, a_shape):
        return dict(
            core_in=v((count, D, D), BF16),
            pair=v((4, count) + a_shape, BF16),
            a_in=v((3, count) + a_shape, BF16),
            a_sum=v((count,) + a_shape, BF16),
            b_in=v((3, count, 128, 128), BF16),
            b_sum=v((count, 128, 128), BF16),
            z_in=v((ZN - 1, count, 16, 128), BF16),
            core_sems=pair(count),
            a_sems=pair(3, count),
            b_sems=pair(3),
            z_sems=pair(ZN - 1),
            dp_sems=(dma((7,)), dma((YN,))),
        )

    return dict(
        edges=v((EDGES, D), BF16),
        edge_first=v((3, D, D), BF16),
        edge_second=v((D, D), BF16),
        node_first=v((2, D, D), BF16),
        node_second=v((D, D), BF16),
        node_cot=v((ND, D), BF16),
        edge_cot=v((EDGES, D), BF16),
        load_sem=dma((7,)),
        store_sem=dma((3,)),
        ring=v((ZN, ND, D), BF16),
        stage=v((ZN, XN, SLOTS, D), BF16),
        buf=v((GN, SLOTS, D), BF16),
        lists_own=v((XN, ZN, ND), F32),
        lists_in=v((XN - 1, ZN, ND), F32),
        lists=v((ZN, ND), jnp.int32),
        perm=v((EDGES, EDGES), BF16),
        perm_back=v((EDGES, EDGES), BF16),
        hot=v((EDGES, ND), BF16),
        hot_back=v((ND, EDGES), BF16),
        h_recv=v((ND, D), BF16),
        act=v((EDGES, D), BF16),
        slope=v((EDGES, D), F32),
        normed=v((EDGES, D), F32),
        inverse=v((EDGES, 1), F32),
        new_edges=v((EDGES, D), BF16),
        new_nodes=v((ND, D), BF16),
        edge_grad=v((EDGES, D), BF16),
        node_part=v((ND, D), F32),
        dz=v((EDGES, D), BF16),
        dpre=v((EDGES, D), BF16),
        back=v((GN, SLOTS, D), BF16),
        rows_in=v((ZN, XN, SLOTS, D), BF16),
        ring_out=v((ZN, ND, D), BF16),
        ring_in=v((ZN, ND, D), BF16),
        grads=v((7, D, D), BF16),
        sums=v((4, 8, D), F32),
        dp_sums=v((7, 8, D), F32),
        x_sums=v((XN - 1, 8, D), F32),
        z_sums=v((ZN - 1, 8, D), F32),
        hop_sems=pair(ZN, PARTS),
        list_sems=pair(XN - 1),
        away_sems=pair(ZN, XN - 1),
        row_sems=pair(ZN, XN - 1),
        back_sems=pair(ZN, PARTS),
        sdp_sems=pair(7),
        sx_sems=pair(XN - 1),
        sz_sems=pair(ZN - 1),
        edge_share=share(4, (D, 128)),
        node_share=share(3, (128, D)),
    )


def layer(counts, node, senders, recv, vectors, edges, edge_first, edge_second, node_first, node_second, node_cot, edge_cot):
    vmem = pl.BlockSpec(memory_space=pltpu.VMEM)
    hbm = pl.BlockSpec(memory_space=pl.ANY)
    return pl.pallas_call(
        layer_kernel,
        out_shape=(
            jax.ShapeDtypeStruct((ND, D), BF16),
            jax.ShapeDtypeStruct((EDGES, D), BF16),
            jax.ShapeDtypeStruct((EDGES, D), BF16),
            jax.ShapeDtypeStruct((ND, D), BF16),
            jax.ShapeDtypeStruct((YN, 4, 16, 128), BF16),
            jax.ShapeDtypeStruct((YN, 3, 16, 128), BF16),
            jax.ShapeDtypeStruct((8, D), F32),
        ),
        in_specs=[pl.BlockSpec(memory_space=pltpu.SMEM)] + [vmem] * 4 + [hbm] * 7,
        out_specs=(hbm,) * 3 + (vmem,) * 4,
        scratch_shapes=[scratch()],
        compiler_params=pltpu.CompilerParams(
            collective_id=0, has_side_effects=True, vmem_limit_bytes=VMEM_LIMIT
        ),
        name="layer",
    )(counts, node, senders, recv, vectors, edges, edge_first, edge_second, node_first, node_second, node_cot, edge_cot)


def outputs_kernel(
    nodes_in,
    edges_in,
    edge_grad_in,
    node_grad_in,
    edge_part,
    node_part,
    sums_ref,
    nodes_out,
    edges_out,
    edge_grad_out,
    node_grad_out,
    edge_first_ref,
    edge_second_ref,
    node_first_ref,
    node_second_ref,
    vectors_ref,
    edges_held,
    edge_grad_held,
    nodes_held,
    node_grad_held,
    in_sems,
    out_sems,
):
    moves = []
    for src, held, dst in (
        (edges_in, edges_held, edges_out),
        (edge_grad_in, edge_grad_held, edge_grad_out),
        (nodes_in, nodes_held, nodes_out),
        (node_grad_in, node_grad_held, node_grad_out),
    ):
        size = min(CHUNK, src.shape[0])
        for first in range(0, src.shape[0], size):
            piece, index = pl.ds(first, size), len(moves)
            moves.append(
                (
                    pltpu.make_async_copy(src.at[piece], held.at[piece], in_sems.at[index]),
                    pltpu.make_async_copy(held.at[piece], dst.at[piece], out_sems.at[index]),
                )
            )
    for fetch, _ in moves:
        fetch.start()
    for j in range(YN):
        lanes = slice(j * 128, (j + 1) * 128)
        for m in range(3):
            edge_first_ref[m, :, lanes] = edge_part[j, m].astype(F32)
        edge_second_ref[:, lanes] = edge_part[j, 3].astype(F32)
        for m in range(2):
            node_first_ref[m, :, lanes] = node_part[j, m].astype(F32)
        node_second_ref[:, lanes] = node_part[j, 2].astype(F32)
    shift = (D - lax.axis_index("graph") * 16) % D
    vectors_ref[...] = pltpu.roll(sums_ref[...], shift, 1)[0:4, 0:16]
    for fetch, store in moves:
        fetch.wait()
        store.start()
    for _, store in moves:
        store.wait()


def outputs(nodes, edges, edge_grad, node_grad, edge_part, node_part, sums):
    vmem = pl.BlockSpec(memory_space=pltpu.VMEM)
    hbm = pl.BlockSpec(memory_space=pl.ANY)
    return pl.pallas_call(
        outputs_kernel,
        out_shape=(
            jax.ShapeDtypeStruct((ND, D), BF16),
            jax.ShapeDtypeStruct((EDGES, D), BF16),
            jax.ShapeDtypeStruct((EDGES, D), BF16),
            jax.ShapeDtypeStruct((ND, D), BF16),
            jax.ShapeDtypeStruct((3, 16, D), F32),
            jax.ShapeDtypeStruct((16, D), F32),
            jax.ShapeDtypeStruct((2, 16, D), F32),
            jax.ShapeDtypeStruct((16, D), F32),
            jax.ShapeDtypeStruct((4, 16), F32),
        ),
        in_specs=[hbm] * 4 + [vmem] * 3,
        out_specs=(hbm,) * 4 + (vmem,) * 5,
        scratch_shapes=[
            pltpu.VMEM((EDGES, D), BF16),
            pltpu.VMEM((EDGES, D), BF16),
            pltpu.VMEM((ND, D), BF16),
            pltpu.VMEM((ND, D), BF16),
            pltpu.SemaphoreType.DMA((2 * EDGES // CHUNK + 2,)),
            pltpu.SemaphoreType.DMA((2 * EDGES // CHUNK + 2,)),
        ],
        compiler_params=pltpu.CompilerParams(vmem_limit_bytes=VMEM_LIMIT),
        name="outputs",
    )(nodes, edges, edge_grad, node_grad, edge_part, node_part, sums)


def body(
    node_latents,
    edge_latents,
    senders,
    receivers,
    block_counts,
    edge_first,
    edge_second,
    node_first,
    node_second,
    vectors,
    node_cotangent,
    edge_cotangent,
):
    new_nodes, new_edges, edge_grad, node_grad, edge_part, node_part, sums = layer(
        block_counts,
        node_latents[0],
        senders,
        receivers,
        vectors,
        edge_latents.reshape(EDGES, D),
        edge_first,
        edge_second,
        node_first,
        node_second,
        node_cotangent[0],
        edge_cotangent.reshape(EDGES, D),
    )
    new_nodes, new_edges, edge_grad, node_grad, grad_ef, grad_es, grad_nf, grad_ns, columns = outputs(
        new_nodes, new_edges, edge_grad, node_grad, edge_part, node_part, sums
    )
    shape = edge_latents.shape
    return (
        new_nodes[None],
        new_edges.reshape(shape),
        node_grad[None],
        edge_grad.reshape(shape),
        grad_ef,
        grad_es,
        grad_nf,
        grad_ns,
        columns,
    )


def solution(mesh):
    return jax.shard_map(
        body,
        mesh=mesh,
        in_specs=(
            P("dp", "graph", None),
            P("dp", "graph", None, None),
            P("graph", None),
            P("graph", None),
            P("graph"),
            P(),
            P(),
            P(),
            P(),
            P(),
            P("dp", "graph", None),
            P("dp", "graph", None, None),
        ),
        out_specs=(
            P("dp", "graph", None),
            P("dp", "graph", None, None),
            P("dp", "graph", None),
            P("dp", "graph", None, None),
            P(None, "graph", None),
            P("graph", None),
            P(None, "graph", None),
            P("graph", None),
            P(None, "graph"),
        ),
        check_vma=False,
    )
```

time: 860 us -> 90.9 us (0.11)
  waiting for transfers between devices: 726 us -> 0 us
  Pallas kernels: 0 us -> 89.3 us
  matrix products: 36.1 us -> 0 us
  other arithmetic: 33.9 us -> 0 us
  local copies, waits for them, and re-layouts: 26.5 us -> 0 us
  blocking collectives: 17.9 us -> 0 us
  between operations: 14.8 us -> 1.46 us
    reduce_scatter x2 -> x0, waiting for transfers between devices: 431 us -> none  [the longest x1 216 us: body(): lax.psum_scatter(dense_send.astype(jnp.bfloat16), 'graph', scatter_dimens...]
    unnamed x6 -> x0, waiting for transfers between devices: 170 us -> none
    pallas_call x0 -> x2, Pallas kernels: none -> 89.3 us  [the longest x1 85.2 us: layer(): pl.pallas_call(layer_kernel, out_shape=(jax.ShapeDtypeStruct((ND, D), BF1...]
    all_gather x1 -> x0, waiting for transfers between devices: 76.3 us -> none  [body(): all_nodes = lax.all_gather(node_latents, 'graph', axis=1, tiled=True)[0]]
    psum x1 -> x0, waiting for transfers between devices: 49.1 us -> none  [body(): lax.psum(matrices.astype(jnp.bfloat16), 'dp').astype(jnp.float32)]
    dot_general x23 -> x0, matrix products: 36.1 us -> none  [the longest x6 11.2 us: product_back(): lax.dot_general(left, right, (((1,), (1,)), ((), ())), preferred_element_...]
    psum x1 -> x0, blocking collectives: 17.9 us -> none  [body(): lax.psum(columns.astype(jnp.bfloat16), 'dp').astype(jnp.float32)]
    scatter-add x2 -> x0, other arithmetic: 17.7 us -> none  [the longest x1 11 us: body(): jax.ops.segment_sum(product_back(edge_dpre, edge_first[1]), send_index, n...]
  transfers between devices with their start and end apart: 5 -> 0, of which waited for: 5 -> 0; matrix products, arithmetic and copies ran while one was open for 5% -> 0% of each run, Pallas kernels for 0% -> 0%
where the time goes in v2:
time: 90.9 us; the launch traced here: 90.7 us
  Pallas kernels  89.3 us (98%)
  between operations  1.46 us (2%)
    pallas_call x1, Pallas kernels, layer(): pl.pallas_call(layer_kernel, out_shape=(jax.ShapeDtypeStruct((ND, D), BF1...  85.2 us
    pallas_call x1, Pallas kernels, outputs(): pl.pallas_call(outputs_kernel, out_shape=(jax.ShapeDtypeStruct((ND, D), B...  4.07 us

profile of v2, /device:TPU:1, one launch (start us, length us, event | category | flops | bytes accessed | tf_op | source)
XLA Modules:
  0.0 90.7 jit_solution(8083936668147648871)
XLA Ops:
  1.3 85.2 %layer.1 = (bf16[128,512]{1,0:T(8,128)(2,1)}, bf16[1024,512]{1,0:T(8,128)(2,1)}, bf16[1024,512]{1,0:T(8,128)(2,1)}, bf16[128,512]{1,0:T(8,128)(2,1)}, bf16[4,4,1...) custom-call(s32[1]{0:T(128)S(6)} %copy.21.counts_ref, bf16[128,512]{1,0:T(8,128)(2,1)} %bitcast.10, ...), custom_call_target="tpu_custom_call" | custom-call | tf_op jit(solution)/shard_map/layer/pallas_call | solution.py:658
  86.5 4.1 %outputs.1 = (bf16[128,512]{1,0:T(8,128)(2,1)}, bf16[1024,512]{1,0:T(8,128)(2,1)}, bf16[1024,512]{1,0:T(8,128)(2,1)}, bf16[128,512]{1,0:T(8,128)(2,1)}, f32[3,16...) custom-call(bf16[128,512]{1,0:T(8,128)(2,1)} %get-tuple-element.25.nodes_, ...), custom_call_target="tpu_custom_call" | custom-call | tf_op jit(solution)/shard_map/outputs/pallas_call | solution.py:741

commit v3 on v2

--- a/solution.py
+++ b/solution.py
@@ -18,7 +18,7 @@
 D = 512
 EDGES = 1024
 SLOTS = 32
-BM = 256
+BM = 512
 NB = EDGES // BM
 VMEM_LIMIT = 56 * 1024 * 1024
 
@@ -48,13 +48,6 @@
     return pltpu.make_async_remote_copy(
         src_ref=src, dst_ref=dst, send_sem=send, recv_sem=recv, device_id=device, device_id_type=MESH
     )
-
-
-def enter(devices):
-    barrier = pltpu.get_barrier_semaphore()
-    for device in devices:
-        pl.semaphore_signal(barrier, inc=1, device_id=device, device_id_type=MESH)
-    pl.semaphore_wait(barrier, len(devices))
 
 
 def onehot_rows(count, row):
@@ -100,10 +93,10 @@
 
 def layer_kernel(
     counts_ref,
-    node_ref,
-    senders_ref,
-    recv_ref,
-    vectors_ref,
+    node_hbm,
+    senders_hbm,
+    recv_hbm,
+    vectors_hbm,
     edge_hbm,
     edge_first_hbm,
     edge_second_hbm,
@@ -131,6 +124,12 @@
     dp_peers = [None] + [((dp + k) % 8, graph) for k in range(1, 8)]
     up, down = z_peers[1], z_peers[ZN - 1]
 
+    peers = x_peers[1:] + z_peers[1:] + dp_peers[1:]
+    barrier = pltpu.get_barrier_semaphore()
+    for device in peers:
+        pl.semaphore_signal(barrier, inc=1, device_id=device, device_id_type=MESH)
+
+    node_ref, senders_ref, recv_ref, vectors_ref = s.node, s.senders, s.recv, s.vectors
     loads = {}
     for index, (hbm, ref) in enumerate(
         (
@@ -141,15 +140,21 @@
             (node_second_hbm, s.node_second),
             (node_cot_hbm, s.node_cot),
             (edge_cot_hbm, s.edge_cot),
+            (node_hbm, s.node),
+            (senders_hbm, s.senders),
+            (recv_hbm, s.recv),
+            (vectors_hbm, s.vectors),
         )
     ):
         loads[index] = pltpu.make_async_copy(hbm, ref, s.load_sem.at[index])
+    for index in (7, 8, 9, 10, 0, 1, 2, 3, 4, 5, 6):
         loads[index].start()
     edges, edge_first, edge_second = s.edges, s.edge_first, s.edge_second
     node_first, node_second = s.node_first, s.node_second
     edge_cot, node_cot = s.edge_cot, s.node_cot
 
-    enter(x_peers[1:] + z_peers[1:] + dp_peers[1:])
+    loads[7].wait()
+    pl.semaphore_wait(barrier, len(peers))
     sent = []
 
     def start(src, dst, sems, index, device):
@@ -170,6 +175,8 @@
         hops[1, part] = hop(node_ref, 1, up, part)
         hops[5, part] = hop(node_ref, 5, down, part)
 
+    for index in (8, 9, 10):
+        loads[index].wait()
     senders = senders_ref[...]
     owners = senders // ND
     local = (senders % ND).astype(F32)
@@ -225,10 +232,12 @@
 
     def forward(slot, part):
         hops[slot, part].wait_recv()
-        if slot in (1, 2, 3):
+        if slot in (1, 2) or (slot == 3 and part == 0):
             hops[slot + 1, part] = hop(ring.at[slot], slot + 1, up, part)
         elif slot in (5, 6):
             hops[slot + 1, part] = hop(ring.at[slot], slot + 1, down, part)
+        elif slot == 7 and part == 1:
+            hops[4, part] = hop(ring.at[slot], 4, down, part)
 
     def relay(slot):
         source = (z + RING_OFFSET[slot] + ZN) % ZN
@@ -458,7 +467,7 @@
         hat = normed[rows, :]
         col_scale = col_scale + jnp.sum(message_cot * hat, 0, keepdims=True)
         dz[rows, :] = norm_backward(message_cot, hat, inverse[rows, :], vectors_ref[2:3, :]).astype(BF16)
-        if i == NB // 2 - 1:
+        if i == 0:
             for m in range(3):
                 node_share.across_a(m)
     grads[3] = tn(act[...], dz[...]).astype(BF16)
@@ -471,8 +480,9 @@
         dpre[rows, :] = dpre_b
         col_edge = col_edge + jnp.sum(dpre_b.astype(F32), 0, keepdims=True)
         received = received + nn(hot_back[:, rows], dpre_b)
+        if i == 0:
+            edge_share.across_a(3)
     received = received.astype(BF16)
-    edge_share.across_a(3)
     grads[2] = tn(h, received).astype(BF16)
     edge_share.give(2)
     grads[0] = tn(edges[...], dpre[...]).astype(BF16)
@@ -488,9 +498,9 @@
             for k in range(1, XN)
         ]
     edge_share.across_a(2)
+    edge_share.across_a(0)
     grads[1] = tn(buf[...].reshape(EDGES, D), back[...].reshape(EDGES, D)).astype(BF16)
     edge_share.give(1)
-    edge_share.across_a(0)
 
     sums = s.sums
     sums[0] = jnp.concatenate([col_edge, col_node, col_scale, col_node_scale, jnp.zeros((4, D), F32)], axis=0)
@@ -498,8 +508,6 @@
     for j in REDUCE_ORDER:
         target = (z + REDUCE_OFFSET[j] + ZN) % ZN
         rows_in[j, x] = back[x * ZN + target]
-    edge_share.across_a(1)
-    node_share.across_b()
 
     ring_out, ring_in = s.ring_out, s.ring_in
     ring_copies = {}
@@ -513,12 +521,13 @@
             for part in range(PARTS):
                 piece = slice(part * rows_of, (part + 1) * rows_of)
                 partial = total[piece]
-                if j in (3, 2, 1, 6, 5):
-                    ring_copies[j + 1, part].wait_recv()
-                    partial = partial + ring_in[j + 1, piece].astype(F32)
+                before = j + 1 if j in (2, 1, 6, 5) or (j == 3 and part == 0) else 4 if j == 7 and part == 1 else None
+                if before:
+                    ring_copies[before, part].wait_recv()
+                    partial = partial + ring_in[before, piece].astype(F32)
                 ring_out[j, piece] = partial.astype(BF16)
                 ring_copies[j, part] = start(
-                    ring_out.at[j, piece], ring_in.at[j, piece], s.back_sems, (j, part), up if j < 5 else down
+                    ring_out.at[j, piece], ring_in.at[j, piece], s.back_sems, (j, part), up if j < 4 or (j == 4 and part == 0) else down
                 )
             return
         for part in range(PARTS):
@@ -539,10 +548,12 @@
     for i in range(NB):
         rows = slice(i * BM, (i + 1) * BM)
         edge_grad[rows, :] = (edge_cot[rows, :].astype(F32) + nt(dpre[rows, :], edge_first[0])).astype(BF16)
-        if i % 2:
-            ring_step(REDUCE_ORDER[i // 2])
+        if i == 0:
+            edge_share.across_a(1)
+        ring_step(REDUCE_ORDER[i])
     store_grad = pltpu.make_async_copy(edge_grad, edge_grad_hbm, s.store_sem.at[2])
     store_grad.start()
+    node_share.across_b()
     for copy in dp_sums:
         copy.wait_recv()
     sum_step(s.dp_sums, 0, 1)
@@ -550,29 +561,29 @@
     ring_step(3)
     ring_step(6)
     node_share.across_z()
+    edge_share.across_b()
     ring_step(2)
     ring_step(5)
-    edge_share.across_b()
+    node_share.across_dp()
+    edge_share.across_z()
     for copy in x_sums:
         copy.wait_recv()
     sum_step(s.x_sums, 1, 2)
     z_sums = [start(sums.at[2], s.z_sums.at[k - 1], s.sz_sems, k - 1, z_peers[k]) for k in range(1, ZN)]
     ring_step(1)
-    node_share.across_dp()
-    edge_share.across_z()
+    edge_share.across_dp()
     ring_step(0)
     for copy in z_sums:
         copy.wait_recv()
     sum_step(s.z_sums, 2, 3)
     sums_ref[...] = sums[3]
-    node_share.finish()
-    edge_share.across_dp()
     store_edges.wait()
     store_nodes.wait()
     store_grad.wait()
     for copy in sent:
         copy.wait_send()
     edge_share.finish()
+    node_share.finish()
     node_share.drain()
     edge_share.drain()
 
@@ -607,7 +618,11 @@
         node_second=v((D, D), BF16),
         node_cot=v((ND, D), BF16),
         edge_cot=v((EDGES, D), BF16),
-        load_sem=dma((7,)),
+        load_sem=dma((11,)),
+        node=v((ND, D), BF16),
+        senders=v((8, 128), jnp.int32),
+        recv=v((8, 128), jnp.int32),
+        vectors=v((4, D), F32),
         store_sem=dma((3,)),
         ring=v((ZN, ND, D), BF16),
         stage=v((ZN, XN, SLOTS, D), BF16),
@@ -666,7 +681,7 @@
             jax.ShapeDtypeStruct((YN, 3, 16, 128), BF16),
             jax.ShapeDtypeStruct((8, D), F32),
         ),
-        in_specs=[pl.BlockSpec(memory_space=pltpu.SMEM)] + [vmem] * 4 + [hbm] * 7,
+        in_specs=[pl.BlockSpec(memory_space=pltpu.SMEM)] + [hbm] * 11,
         out_specs=(hbm,) * 3 + (vmem,) * 4,
         scratch_shapes=[scratch()],
         compiler_params=pltpu.CompilerParams(

time: 90.9 us -> 85 us (0.935)
  Pallas kernels: 89.3 us -> 83.3 us
    pallas_call x1, Pallas kernels: 85.2 us -> 79.3 us  [layer(): pl.pallas_call(layer_kernel, out_shape=(jax.ShapeDtypeStruct((ND, D), BF1...]
where the time goes in v3:
time: 85 us; the launch traced here: 84.8 us
  Pallas kernels  83.3 us (98%)
  between operations  1.46 us (2%)
    pallas_call x1, Pallas kernels, layer(): pl.pallas_call(layer_kernel, out_shape=(jax.ShapeDtypeStruct((ND, D), BF1...  79.3 us
    pallas_call x1, Pallas kernels, outputs(): pl.pallas_call(outputs_kernel, out_shape=(jax.ShapeDtypeStruct((ND, D), B...  4.07 us

profile of v3, /device:TPU:1, one launch (start us, length us, event | category | flops | bytes accessed | tf_op | source)
XLA Modules:
  0.0 84.8 jit_solution(2283667331339983551)
XLA Ops:
  1.3 79.3 %layer.1 = (bf16[128,512]{1,0:T(8,128)(2,1)}, bf16[1024,512]{1,0:T(8,128)(2,1)}, bf16[1024,512]{1,0:T(8,128)(2,1)}, bf16[128,512]{1,0:T(8,128)(2,1)}, bf16[4,4,1...) custom-call(s32[1]{0:T(128)S(6)} %copy.21.counts_ref, bf16[128,512]{1,0:T(8,128)(2,1)} %bitcast.10, ...), custom_call_target="tpu_custom_call" | custom-call | tf_op jit(solution)/shard_map/layer/pallas_call | solution.py:673
  80.6 4.1 %outputs.1 = (bf16[128,512]{1,0:T(8,128)(2,1)}, bf16[1024,512]{1,0:T(8,128)(2,1)}, bf16[1024,512]{1,0:T(8,128)(2,1)}, bf16[128,512]{1,0:T(8,128)(2,1)}, f32[3,16...) custom-call(bf16[128,512]{1,0:T(8,128)(2,1)} %get-tuple-element.25.nodes_, ...), custom_call_target="tpu_custom_call" | custom-call | tf_op jit(solution)/shard_map/outputs/pallas_call | solution.py:756

commit v4 on v3

--- a/solution.py
+++ b/solution.py
@@ -79,6 +79,7 @@
 REDUCE_OFFSET = (0, 1, 2, 3, 4, -1, -2, -3)
 PARTS = 2
 CHUNK = 256
+FILL = EDGES // 4
 
 
 def hot_columns(column, count):
@@ -214,10 +215,9 @@
             s.h_recv[...] = nn(h, edge_first[2]).astype(BF16)
         elif step == 1:
             loads[1].wait()
-        if 1 <= step <= NB:
-            i = step - 1
-            rows = slice(i * BM, (i + 1) * BM)
-            for b in range(i * BM // 128, (i + 1) * BM // 128):
+        if step:
+            rows = slice((step - 1) * FILL, step * FILL)
+            for b in range((step - 1) * FILL // 128, step * FILL // 128):
                 block = slice(b * 128, (b + 1) * 128)
                 perm[block, :] = hot_columns(slot_columns[:, b : b + 1], EDGES)
                 perm_back[:, block] = onehot_rows(EDGES, slot_rows[b])
@@ -483,10 +483,6 @@
         if i == 0:
             edge_share.across_a(3)
     received = received.astype(BF16)
-    grads[2] = tn(h, received).astype(BF16)
-    edge_share.give(2)
-    grads[0] = tn(edges[...], dpre[...]).astype(BF16)
-    edge_share.give(0)
     back = s.back
     back[...] = nn(perm_back[...], dpre[...]).astype(BF16).reshape(GN, SLOTS, D)
     rows_in = s.rows_in
@@ -497,6 +493,10 @@
             start(back.at[((x + k) % XN) * ZN + target], rows_in.at[j, x], s.row_sems, (j, k - 1), x_peers[k])
             for k in range(1, XN)
         ]
+    grads[2] = tn(h, received).astype(BF16)
+    edge_share.give(2)
+    grads[0] = tn(edges[...], dpre[...]).astype(BF16)
+    edge_share.give(0)
     edge_share.across_a(2)
     edge_share.across_a(0)
     grads[1] = tn(buf[...].reshape(EDGES, D), back[...].reshape(EDGES, D)).astype(BF16)
@@ -691,37 +691,12 @@
     )(counts, node, senders, recv, vectors, edges, edge_first, edge_second, node_first, node_second, node_cot, edge_cot)
 
 
-def outputs_kernel(
-    nodes_in,
-    edges_in,
-    edge_grad_in,
-    node_grad_in,
-    edge_part,
-    node_part,
-    sums_ref,
-    nodes_out,
-    edges_out,
-    edge_grad_out,
-    node_grad_out,
-    edge_first_ref,
-    edge_second_ref,
-    node_first_ref,
-    node_second_ref,
-    vectors_ref,
-    edges_held,
-    edge_grad_held,
-    nodes_held,
-    node_grad_held,
-    in_sems,
-    out_sems,
-):
+def outputs_kernel(*refs):
+    copied_in, parts_in, copied_out, small_out = refs[0:4], refs[4:7], refs[7:11], refs[11:16]
+    copied, parts, small = refs[16:20], refs[20:23], refs[23:28]
+    in_sems, out_sems, part_sems, small_sems = refs[28:32]
     moves = []
-    for src, held, dst in (
-        (edges_in, edges_held, edges_out),
-        (edge_grad_in, edge_grad_held, edge_grad_out),
-        (nodes_in, nodes_held, nodes_out),
-        (node_grad_in, node_grad_held, node_grad_out),
-    ):
+    for src, held, dst in zip(copied_in, copied, copied_out):
         size = min(CHUNK, src.shape[0])
         for first in range(0, src.shape[0], size):
             piece, index = pl.ds(first, size), len(moves)
@@ -731,8 +706,16 @@
                     pltpu.make_async_copy(held.at[piece], dst.at[piece], out_sems.at[index]),
                 )
             )
+    loads = [pltpu.make_async_copy(src, held, part_sems.at[i]) for i, (src, held) in enumerate(zip(parts_in, parts))]
+    stores = [pltpu.make_async_copy(held, dst, small_sems.at[i]) for i, (held, dst) in enumerate(zip(small, small_out))]
+    for load in loads:
+        load.start()
     for fetch, _ in moves:
         fetch.start()
+    for load in loads:
+        load.wait()
+    edge_part, node_part, sums_ref = parts
+    edge_first_ref, edge_second_ref, node_first_ref, node_second_ref, vectors_ref = small
     for j in range(YN):
         lanes = slice(j * 128, (j + 1) * 128)
         for m in range(3):
@@ -743,42 +726,34 @@
         node_second_ref[:, lanes] = node_part[j, 2].astype(F32)
     shift = (D - lax.axis_index("graph") * 16) % D
     vectors_ref[...] = pltpu.roll(sums_ref[...], shift, 1)[0:4, 0:16]
+    for store in stores:
+        store.start()
     for fetch, store in moves:
         fetch.wait()
         store.start()
     for _, store in moves:
         store.wait()
+    for store in stores:
+        store.wait()
 
 
 def outputs(nodes, edges, edge_grad, node_grad, edge_part, node_part, sums):
-    vmem = pl.BlockSpec(memory_space=pltpu.VMEM)
     hbm = pl.BlockSpec(memory_space=pl.ANY)
-    return pl.pallas_call(
+    copied = [((EDGES, D), BF16), ((EDGES, D), BF16), ((ND, D), BF16), ((ND, D), BF16)]
+    parts = [((YN, 4, 16, 128), BF16), ((YN, 3, 16, 128), BF16), ((8, D), F32)]
+    small = [((3, 16, D), F32), ((16, D), F32), ((2, 16, D), F32), ((16, D), F32), ((4, 16), F32)]
+    moves = 2 * EDGES // CHUNK + 2
+    new_edges, edge_grad, new_nodes, node_grad, *rest = pl.pallas_call(
         outputs_kernel,
-        out_shape=(
-            jax.ShapeDtypeStruct((ND, D), BF16),
-            jax.ShapeDtypeStruct((EDGES, D), BF16),
-            jax.ShapeDtypeStruct((EDGES, D), BF16),
-            jax.ShapeDtypeStruct((ND, D), BF16),
-            jax.ShapeDtypeStruct((3, 16, D), F32),
-            jax.ShapeDtypeStruct((16, D), F32),
-            jax.ShapeDtypeStruct((2, 16, D), F32),
-            jax.ShapeDtypeStruct((16, D), F32),
-            jax.ShapeDtypeStruct((4, 16), F32),
-        ),
-        in_specs=[hbm] * 4 + [vmem] * 3,
-        out_specs=(hbm,) * 4 + (vmem,) * 5,
-        scratch_shapes=[
-            pltpu.VMEM((EDGES, D), BF16),
-            pltpu.VMEM((EDGES, D), BF16),
-            pltpu.VMEM((ND, D), BF16),
-            pltpu.VMEM((ND, D), BF16),
-            pltpu.SemaphoreType.DMA((2 * EDGES // CHUNK + 2,)),
-            pltpu.SemaphoreType.DMA((2 * EDGES // CHUNK + 2,)),
-        ],
+        out_shape=tuple(jax.ShapeDtypeStruct(*one) for one in copied + small),
+        in_specs=[hbm] * 7,
+        out_specs=(hbm,) * 9,
+        scratch_shapes=[pltpu.VMEM(*one) for one in copied + parts + small]
+        + [pltpu.SemaphoreType.DMA((count,)) for count in (moves, moves, 3, 5)],
         compiler_params=pltpu.CompilerParams(vmem_limit_bytes=VMEM_LIMIT),
         name="outputs",
-    )(nodes, edges, edge_grad, node_grad, edge_part, node_part, sums)
+    )(edges, edge_grad, nodes, node_grad, edge_part, node_part, sums)
+    return new_nodes, new_edges, edge_grad, node_grad, *rest
 
 
 def body(

time: 85 us -> 83.6 us (0.984)
  Pallas kernels: 83.3 us -> 82 us
    pallas_call x1, Pallas kernels: 4.07 us -> 3.18 us  [outputs(): pl.pallas_call(outputs_kernel, out_shape=tuple((jax.ShapeDtypeStruct(*one...]
where the time goes in v4:
time: 83.6 us; the launch traced here: 83.5 us
  Pallas kernels  82 us (98%)
  between operations  1.46 us (2%)
    pallas_call x1, Pallas kernels, layer(): pl.pallas_call(layer_kernel, out_shape=(jax.ShapeDtypeStruct((ND, D), BF1...  78.8 us
    pallas_call x1, Pallas kernels, outputs(): pl.pallas_call(outputs_kernel, out_shape=tuple((jax.ShapeDtypeStruct(*one...  3.18 us

profile of v4, /device:TPU:1, one launch (start us, length us, event | category | flops | bytes accessed | tf_op | source)
XLA Modules:
  0.0 83.5 jit_solution(14495246322820702341)
XLA Ops:
  1.3 78.8 %layer.1 = (bf16[128,512]{1,0:T(8,128)(2,1)}, bf16[1024,512]{1,0:T(8,128)(2,1)}, bf16[1024,512]{1,0:T(8,128)(2,1)}, bf16[128,512]{1,0:T(8,128)(2,1)}, bf16[4,4,1...) custom-call(s32[1]{0:T(128)S(6)} %copy.21.counts_ref, bf16[128,512]{1,0:T(8,128)(2,1)} %bitcast.10, ...), custom_call_target="tpu_custom_call" | custom-call | tf_op jit(solution)/shard_map/layer/pallas_call | solution.py:673
  80.1 3.2 %outputs.1 = (bf16[1024,512]{1,0:T(8,128)(2,1)}, bf16[1024,512]{1,0:T(8,128)(2,1)}, bf16[128,512]{1,0:T(8,128)(2,1)}, bf16[128,512]{1,0:T(8,128)(2,1)}, f32[3,16...) custom-call(bf16[1024,512]{1,0:T(8,128)(2,1)} %get-tuple-element.25.refs_, ...), custom_call_target="tpu_custom_call" | custom-call | tf_op jit(solution)/shard_map/outputs/pallas_call | solution.py:746

commit v5 on v4

--- a/solution.py
+++ b/solution.py
@@ -553,13 +553,13 @@
         ring_step(REDUCE_ORDER[i])
     store_grad = pltpu.make_async_copy(edge_grad, edge_grad_hbm, s.store_sem.at[2])
     store_grad.start()
+    ring_step(3)
     node_share.across_b()
+    ring_step(6)
     for copy in dp_sums:
         copy.wait_recv()
     sum_step(s.dp_sums, 0, 1)
     x_sums = [start(sums.at[1], s.x_sums.at[k - 1], s.sx_sems, k - 1, x_peers[k]) for k in range(1, XN)]
-    ring_step(3)
-    ring_step(6)
     node_share.across_z()
     edge_share.across_b()
     ring_step(2)

time: 83.6 us -> 83.5 us (level)
  no operation moved by 1% of the time
where the time goes in v5:
time: 83.5 us; the launch traced here: 83.3 us
  Pallas kernels  81.9 us (98%)
  between operations  1.46 us (2%)
    pallas_call x1, Pallas kernels, layer(): pl.pallas_call(layer_kernel, out_shape=(jax.ShapeDtypeStruct((ND, D), BF1...  78.7 us
    pallas_call x1, Pallas kernels, outputs(): pl.pallas_call(outputs_kernel, out_shape=tuple((jax.ShapeDtypeStruct(*one...  3.18 us

profile of v5, /device:TPU:1, one launch (start us, length us, event | category | flops | bytes accessed | tf_op | source)
XLA Modules:
  0.0 83.3 jit_solution(15178184855320908149)
XLA Ops:
  1.3 78.7 %layer.1 = (bf16[128,512]{1,0:T(8,128)(2,1)}, bf16[1024,512]{1,0:T(8,128)(2,1)}, bf16[1024,512]{1,0:T(8,128)(2,1)}, bf16[128,512]{1,0:T(8,128)(2,1)}, bf16[4,4,1...) custom-call(s32[1]{0:T(128)S(6)} %copy.21.counts_ref, bf16[128,512]{1,0:T(8,128)(2,1)} %bitcast.10, ...), custom_call_target="tpu_custom_call" | custom-call | tf_op jit(solution)/shard_map/layer/pallas_call | solution.py:673
  80.0 3.2 %outputs.1 = (bf16[1024,512]{1,0:T(8,128)(2,1)}, bf16[1024,512]{1,0:T(8,128)(2,1)}, bf16[128,512]{1,0:T(8,128)(2,1)}, bf16[128,512]{1,0:T(8,128)(2,1)}, f32[3,16...) custom-call(bf16[1024,512]{1,0:T(8,128)(2,1)} %get-tuple-element.25.refs_, ...), custom_call_target="tpu_custom_call" | custom-call | tf_op jit(solution)/shard_map/outputs/pallas_call | solution.py:746
